TPU v7x, 256 devices: a whole 4x4x8 slice. The times are simulated.
256 devices in a mesh: gz: 4 (over y), gx: 8 (over z), gy: 8 (over x, core).
Axes of the slice: x: 4, y: 4, z: 8, core: 2. Of those that a mesh axis runs over, the one named last changes fastest.
Arguments:
- phases: float32 [4, 32, 128, 1024], P(None, 'gz', 'gx', 'gy'), may hold values from 0 to 1, as said below
- solutes: float32 [3, 32, 128, 1024], P(None, 'gz', 'gx', 'gy'), may hold values from 0 to 1
- melt: float32 [3], replicated, may hold values from 0.2 to 0.6
- shift_rows: int32 [1], replicated, may hold values from 1 to 8
- flags: int32 [4, 8, 8, 32], P('gz', 'gx', 'gy'), may hold values 0 or 1
- balance: int32 [4, 8, 8, 32], P('gz', 'gx', 'gy'), may hold values from 0 to 63, as said below
- stiffness: float32 [4, 3], replicated, may hold values from 0.04 to 0.16
- barrier: float32 [4], replicated, may hold values from 0.5 to 2
- coupling: float32 [4, 3], replicated, may hold values from -2.4 to 2.4
- slope: float32 [4], replicated, may hold values from -1 to 1
- diffusivity: float32 [4, 3], replicated, may hold values from 0.02 to 0.12
- release: float32 [4, 3], replicated, may hold values from -2 to 2
Outputs:
- phases_out: float32 [4, 32, 128, 1024], P(None, 'gz', 'gx', 'gy')
- solutes_out: float32 [3, 32, 128, 1024], P(None, 'gz', 'gx', 'gy')
- moved: float32 [8192, 7, 512], P(('gz', 'gx', 'gy'))
Inputs may be any that keep to these rules, and one draw needn't show every extreme that they name: `phases`: each cell's 4 fractions are nonnegative and sum to one. `balance`: within a growth slab, a device block gives exactly 2 tiles to each owner that it gives any, and every owner receives exactly 32 tiles.
All inputs are finite; a program needn't handle non-finite values. No bound on the sum of `flags` on one device may be relied on, other than what follows from the above.
Results may differ from a plain program's by a relative error of at most 0.0001.
Values sent between devices are 32-bit elements; how exact they have to be, the bound alone decides.
No kernel may reach another device: no remote copies, remote signals or barrier semaphores. Data moves between devices by JAX's collectives and lax.ppermute only.
A program may use at most 64 MiB of HBM per device.

v0:
```python
import jax
import jax.numpy as jnp
from jax import lax
from jax.sharding import PartitionSpec as P

TS = 8
STEPS = 2


def padded(shard, sides, width, wrap):
    for axis, dim in sides:
        devices, length = (lax.axis_size(axis), shard.shape[dim])
        up = [(i, (i + 1) % devices) for i in range(devices if wrap else devices - 1)]
        down = [(j, i) for i, j in up]
        last = lax.slice_in_dim(shard, length - width, length, axis=dim)
        first = lax.slice_in_dim(shard, 0, width, axis=dim)
        before = lax.ppermute(last, axis, up)
        after = lax.ppermute(first, axis, down)
        shard = jnp.concatenate([before, shard, after], axis=dim)
    return shard


def from_behind(value, axis, steps):
    count = lax.axis_size(axis)
    first, last = (max(0, -steps), min(count, count - steps))
    return lax.ppermute(value, axis, [(source, source + steps) for source in range(first, last)])


def column_of(values):
    return values[:, None, None, None]


def melt_column(melt):
    return jnp.concatenate([jnp.array([0.0, 0.0, 0.0, 1.0], dtype=melt.dtype), melt])


def density(fractions, diffusivity):
    summed = column_of(diffusivity[0]) * fractions[0]
    for phase_num in range(1, 4):
        summed = summed + column_of(diffusivity[phase_num]) * fractions[phase_num]
    return summed


def advance(
    fields,
    neighbours,
    flag_cells,
    height,
    stiffness,
    barrier,
    coupling,
    slope,
    diffusivity,
    release,
):
    fractions = fields[:4]
    solute_part = fields[4:]
    laplace = jnp.zeros_like(fractions)
    for axis_num in range(3):
        upper_side, lower_side = neighbours[axis_num]
        laplace = laplace + column_of(stiffness[:, axis_num]) * (
            upper_side[:4] + lower_side[:4] - 2.0 * fractions
        )
    interface = fractions * (1.0 - fractions)
    driving = column_of(slope) * height
    for solute_num in range(3):
        driving = driving + column_of(coupling[:, solute_num]) * solute_part[solute_num]
    growth_rate = flag_cells * (
        laplace + column_of(barrier) * interface * (2.0 * fractions - 1.0) + interface * driving
    )
    change = growth_rate - 0.25 * jnp.sum(growth_rate, axis=0)
    own_density = density(fractions, diffusivity)
    transport = jnp.zeros_like(solute_part)
    for upper_side, lower_side in neighbours:
        for beside in (upper_side, lower_side):
            transport = transport + 0.5 * (own_density + density(beside[:4], diffusivity)) * (
                beside[4:] - solute_part
            )
    released = column_of(release[0]) * change[0]
    for phase_num in range(1, 4):
        released = released + column_of(release[phase_num]) * change[phase_num]
    return jnp.concatenate([fractions + change, solute_part + transport + released], axis=0)


def neighbours_of(fields, at_bottom, at_top):
    side = padded(fields, (("gx", 2), ("gy", 3)), 1, True)
    growth = padded(fields, (("gz", 1),), 1, False)
    low_rim = growth[:, :1]
    high_rim = growth[:, -1:]
    x_upper = side[:, :, 2:, 1:-1]
    x_lower = side[:, :, :-2, 1:-1]
    y_upper = side[:, :, 1:-1, 2:]
    y_lower = side[:, :, 1:-1, :-2]
    low_rim = jnp.where(at_bottom, fields[:, :1], low_rim)
    high_rim = jnp.where(at_top, fields[:, -1:], high_rim)
    z_upper = jnp.concatenate([fields[:, 1:], high_rim], axis=1)
    z_lower = jnp.concatenate([low_rim, fields[:, :-1]], axis=1)
    return [(z_upper, z_lower), (x_upper, x_lower), (y_upper, y_lower)]


def per_device(
    phases,
    solutes,
    melt,
    shift_rows,
    flags,
    balance,
    stiffness,
    barrier,
    coupling,
    slope,
    diffusivity,
    release,
):
    fields = jnp.concatenate([phases, solutes], axis=0)
    components = fields.shape[0]
    depth = fields.shape[1]
    width_x = fields.shape[2]
    width_y = fields.shape[3]
    slab_num = lax.axis_index("gz")
    slab_count = lax.axis_size("gz")
    at_bottom = slab_num == 0
    at_top = slab_num == slab_count - 1
    above = from_behind(fields, "gz", -1)
    incoming = jnp.broadcast_to(column_of(melt_column(melt)), fields.shape)
    above = jnp.where(at_top, incoming, above)
    fields = lax.dynamic_slice_in_dim(
        jnp.concatenate([fields, above], axis=1), shift_rows[0], depth, 1
    )
    tiles_z = depth // TS
    tiles_x = width_x // TS
    tiles_y = width_y // TS
    tile_count = tiles_z * tiles_x * tiles_y
    flag_grid = flags.reshape(tiles_z, tiles_x, tiles_y)
    flag_cells = jnp.repeat(jnp.repeat(jnp.repeat(flag_grid, TS, 0), TS, 1), TS, 2).astype(
        fields.dtype
    )
    row_index = slab_num * depth + jnp.arange(depth)
    height = ((row_index.astype(fields.dtype) + 0.5) / (depth * slab_count) - 0.5).reshape(
        1, depth, 1, 1
    )
    for step_num in range(STEPS):
        fields = advance(
            fields,
            neighbours_of(fields, at_bottom, at_top),
            flag_cells,
            height,
            stiffness,
            barrier,
            coupling,
            slope,
            diffusivity,
            release,
        )
    cube = TS**3
    tiles = fields.reshape(components, tiles_z, TS, tiles_x, TS, tiles_y, TS)
    tiles = tiles.transpose(1, 3, 5, 0, 2, 4, 6).reshape(tile_count, components, cube)
    owner_list = balance.reshape(tile_count)
    rows_x = lax.axis_size("gx")
    rows_y = lax.axis_size("gy")
    owners = rows_x * rows_y
    capacity = max(2, tile_count * 2 // owners)
    serial = jnp.arange(tile_count)
    same_owner = owner_list[:, None] == owner_list[None, :]
    earlier = jnp.sum(
        jnp.logical_and(same_owner, serial[None, :] < serial[:, None]).astype(jnp.int32), axis=1
    )
    slots = owner_list * capacity + earlier
    outgoing = jnp.zeros((owners * capacity, components, cube), fields.dtype).at[slots].set(tiles)
    counts = jnp.sum(
        (owner_list[:, None] == jnp.arange(owners)[None, :]).astype(fields.dtype), axis=0
    )
    arrived, arrived_counts = (
        lax.all_to_all(
            outgoing.reshape(owners, capacity, components, cube),
            ("gx", "gy"),
            split_axis=0,
            concat_axis=0,
            tiled=True,
        ),
        lax.all_to_all(counts, ("gx", "gy"), split_axis=0, concat_axis=0, tiled=True),
    )
    arrived = arrived.reshape(owners * capacity, components, cube)
    received = arrived_counts.astype(jnp.int32)
    starts = jnp.cumsum(received) - received
    within = jnp.arange(capacity)[None, :]
    places = jnp.where(within < received[:, None], starts[:, None] + within, tile_count).reshape(
        owners * capacity
    )
    moved = (
        jnp.zeros((tile_count + 1, components, cube), fields.dtype)
        .at[places]
        .set(arrived)[:tile_count]
    )
    return (fields[:4], fields[4:], moved)


def solution(mesh):
    placed = (
        P(None, "gz", "gx", "gy"),
        P(None, "gz", "gx", "gy"),
        P(),
        P(),
        P("gz", "gx", "gy", None),
        P("gz", "gx", "gy", None),
        P(),
        P(),
        P(),
        P(),
        P(),
        P(),
    )
    return jax.shard_map(
        per_device,
        mesh=mesh,
        in_specs=placed,
        out_specs=(
            P(None, "gz", "gx", "gy"),
            P(None, "gz", "gx", "gy"),
            P(("gz", "gx", "gy"), None, None),
        ),
        check_vma=False,
    )
```

profile of v0, /device:TPU:8, one launch (start us, length us, event | category | flops | bytes accessed | tf_op | source)
XLA Modules:
  0.0 161.1 jit_solution(17807405753161583509)
XLA Ops:
  0.6 1.0 constant_dynamic-update-slice_fusion.1
  1.6 0.9 constant_dynamic-update-slice_fusion
  2.5 4.1 %collective-permute-start = (f32[7,8,16,128]{3,2,1,0:T(8,128)S(1)}, f32[7,8,16,128]{3,2,1,0:T(8,128)S(1)}, u32[]{:S(2)}, u32[]{:S(2)}) collective-permute-start(f32[7,8,16,128]{3,2,1,0:T(8,128)S(1)} %constant_dynamic-update-slice_fusion), channel_id=1, source_target_pairs={{64,0},{128,64},{192,128},{65,1},{129,65},{193,129},{66,2},{130,66... | collective-permute-start | bytes 1376264 | tf_op jit(solution)/shard_map/ppermute | solution.py:26
  8.1 10.5 %all-to-all-start = ((f32[64,1,1]{2,1,0:T(1,128)}), f32[64,1,1]{2,1,0:T(1,128)}, u32[]{:S(2)}, u32[]{:S(2)}) async-start(f32[64,1,1]{2,1,0:T(1,128)} %copy.153), calls=%async_computation | async-start | bytes 65536 | tf_op jit(solution)/shard_map/all_to_all | solution.py:181
  20.3 1.1 fusion.119
  21.5 1.6 slice_reduce_fusion.2
  24.5 1.3 broadcast_multiply_fusion.2
  25.9 1.4 slice_bitcast_fusion.25
  27.6 3.0 %collective-permute-start.3 = (f32[7,8,1,128]{3,1,2,0:T(8,128)S(1)}, f32[7,8,1,128]{3,1,2,0:T(8,128)S(1)}, u32[]{:S(2)}, u32[]{:S(2)}) collective-permute-start(f32[7,8,1,128]{3,1,2,0:T(8,128)S(1)} %bitcast.226), channel_id=1, source_target_pairs={{8,0},{16,8},{24,16},{32,24},{40,32},{48,40},{56,48},{0,56},{9,1},... | collective-permute-start | bytes 86024 | tf_op jit(solution)/shard_map/ppermute | solution.py:18
  31.3 1.9 %collective-permute-start.1 = (f32[7,1,16,128]{3,2,1,0:T(8,128)}, f32[7,1,16,128]{3,2,1,0:T(8,128)}, u32[]{:S(2)}, u32[]{:S(2)}) collective-permute-start(f32[7,1,16,128]{3,2,1,0:T(8,128)} %get-tuple-element.112), channel_id=1, source_target_pairs={{64,0},{128,64},{192,128},{65,1},{129,65},{193,129},{66,2},{130,66... | collective-permute-start | bytes 172040 | tf_op jit(solution)/shard_map/ppermute | solution.py:18
  33.2 3.9 %collective-permute-start.2 = (f32[7,1,16,128]{3,2,1,0:T(8,128)S(1)}, f32[7,1,16,128]{3,2,1,0:T(8,128)}, u32[]{:S(2)}, u32[]{:S(2)}) collective-permute-start(f32[7,1,16,128]{3,2,1,0:T(8,128)S(1)} %get-tuple-element.113), channel_id=1, source_target_pairs={{0,64},{64,128},{128,192},{1,65},{65,129},{129,193},{2,66},{66,130... | collective-permute-start | bytes 172040 | tf_op jit(solution)/shard_map/ppermute | solution.py:17
  38.0 1.6 %collective-permute-start.5 = (f32[7,8,18,1]{2,1,3,0:T(8,128)S(1)}, f32[7,8,18,1]{2,1,3,0:T(8,128)S(1)}, u32[]{:S(2)}, u32[]{:S(2)}) collective-permute-start(f32[7,8,18,1]{2,1,3,0:T(8,128)S(1)} %copy.139), channel_id=1, source_target_pairs={{1,0},{2,1},{3,2},{4,3},{5,4},{6,5},{7,6},{0,7},{9,8},{10,9},{11,1... | collective-permute-start | bytes 12104 | tf_op jit(solution)/shard_map/ppermute | solution.py:18
  41.6 1.0 maximum_bitcast_fusion.23
  42.6 2.7 %collective-permute-done.6 = f32[7,8,18,1]{2,1,3,0:T(8,128)S(1)} collective-permute-done((f32[7,8,18,1]{2,1,3,0:T(8,128)S(1)}, f32[7,8,18,1]{2,1,3,0:T(8,128)S(1)}, u32[]{:S(2)}, u32[]{:S(2)}) %collective-permute-start.6) | collective-permute-done | bytes 4064 | tf_op jit(solution)/shard_map/ppermute | solution.py:17
  50.7 2.8 %collective-permute-start.7 = (f32[7,1,16,128]{3,2,1,0:T(8,128)S(1)}, f32[7,1,16,128]{3,2,1,0:T(8,128)S(1)}, u32[]{:S(2)}, u32[]{:S(2)}) collective-permute-start(f32[7,1,16,128]{3,2,1,0:T(8,128)S(1)} %fusion.115), channel_id=1, source_target_pairs={{64,0},{128,64},{192,128},{65,1},{129,65},{193,129},{66,2},{130,66... | collective-permute-start | bytes 172040 | tf_op jit(solution)/shard_map/ppermute | solution.py:18
  53.5 3.3 %collective-permute-start.9 = (f32[7,8,1,128]{3,1,2,0:T(8,128)S(1)}, f32[7,8,1,128]{3,1,2,0:T(8,128)S(1)}, u32[]{:S(2)}, u32[]{:S(2)}) collective-permute-start(f32[7,8,1,128]{3,1,2,0:T(8,128)S(1)} %bitcast.227), channel_id=1, source_target_pairs={{8,0},{16,8},{24,16},{32,24},{40,32},{48,40},{56,48},{0,56},{9,1},... | collective-permute-start | bytes 86024 | tf_op jit(solution)/shard_map/ppermute | solution.py:18
  59.1 1.3 pad_maximum_fusion.3
  62.6 2.7 %collective-permute-done.12 = f32[7,8,18,1]{2,1,3,0:T(8,128)S(1)} collective-permute-done((f32[7,8,18,1]{2,1,3,0:T(8,128)S(1)}, f32[7,8,18,1]{2,1,3,0:T(8,128)S(1)}, u32[]{:S(2)}, u32[]{:S(2)}) %collective-permute-start.12) | collective-permute-done | bytes 4064 | tf_op jit(solution)/shard_map/ppermute | solution.py:17
  66.9 3.2 %collective-permute-start.8 = (f32[7,1,16,128]{3,2,1,0:T(8,128)S(1)}, f32[7,1,16,128]{3,2,1,0:T(8,128)S(1)}, u32[]{:S(2)}, u32[]{:S(2)}) collective-permute-start(f32[7,1,16,128]{3,2,1,0:T(8,128)S(1)} %get-tuple-element.32), channel_id=1, source_target_pairs={{0,64},{64,128},{128,192},{1,65},{65,129},{129,193},{2,66},{66,130... | collective-permute-start | bytes 172040 | tf_op jit(solution)/shard_map/ppermute | solution.py:17
  70.2 2.8 %collective-permute-done.8 = f32[7,1,16,128]{3,2,1,0:T(8,128)S(1)} collective-permute-done((f32[7,1,16,128]{3,2,1,0:T(8,128)S(1)}, f32[7,1,16,128]{3,2,1,0:T(8,128)S(1)}, u32[]{:S(2)}, u32[]{:S(2)}) %collective-permute-start.8) | collective-permute-done | bytes 57376 | tf_op jit(solution)/shard_map/ppermute | solution.py:17
  73.1 1.5 fusion.121
  76.8 5.8 %reshape.223 = f32[7,1,8,2,8,16,8]{6,5,4,3,2,0,1:T(8,128)} reshape(f32[7,8,16,128]{3,2,1,0:T(8,128)S(1)} %pad_maximum_fusion.5) | data formatting | bytes 917504 | tf_op jit(solution)/shard_map/reshape | solution.py:156
  82.6 7.9 %copy.155 = f32[1,2,16,7,8,8,8]{2,1,6,5,4,3,0:T(2,128)} copy(f32[1,2,16,7,8,8,8]{6,2,5,1,4,3,0:T(8,128)} %bitcast.192) | data formatting | bytes 917504 | tf_op jit(solution)/shard_map/transpose | solution.py:157
  90.5 3.8 %reshape.231 = f32[32,7,512]{0,2,1:T(8,128)S(1)} reshape(f32[1,2,16,7,8,8,8]{2,1,6,5,4,3,0:T(2,128)} %copy.155) | data formatting | bytes 917504 | tf_op jit(solution)/shard_map/reshape | solution.py:157
  95.6 1.5 scatter_fusion
  97.1 2.9 %copy.157 = f32[64,2,7,512]{3,1,2,0:T(2,128)} copy(f32[64,2,7,512]{3,2,1,0:T(8,128)S(1)} %bitcast.193) | data formatting | bytes 3670016 | tf_op jit(solution)/shard_map/reshape | solution.py:175
  100.1 7.6 %all-to-all-start.1 = ((f32[64,2,7,512]{3,1,2,0:T(2,128)}), f32[64,2,7,512]{3,1,2,0:T(2,128)}, u32[]{:S(2)}, u32[]{:S(2)}) async-start(f32[64,2,7,512]{3,1,2,0:T(2,128)} %copy.157), calls=%async_computation.1 | async-start | bytes 3670016 | tf_op jit(solution)/shard_map/all_to_all | solution.py:174
  108.7 2.0 %convert_reduce_fusion.3 = s32[64]{0:T(128)S(1)} fusion(f32[64,1,1]{2,1,0:T(1,128)} %all-to-all-done), kind=kLoop, calls=%fused_computation.308 | loop fusion | flops 64 | bytes 512 | tf_op jit(solution)/shard_map/convert_element_type | solution.py:184
  111.0 42.4 %all-to-all-done.1 = f32[64,2,7,512]{3,1,2,0:T(2,128)} async-done(((f32[64,2,7,512]{3,1,2,0:T(2,128)}), f32[64,2,7,512]{3,1,2,0:T(2,128)}, u32[]{:S(2)}, u32[]{:S(2)}) %all-to-all-start.1) | async-done | bytes 1835040 | tf_op jit(solution)/shard_map/all_to_all | solution.py:174
  153.4 2.0 %copy.161 = f32[64,2,7,512]{3,2,1,0:T(8,128)S(1)} copy(f32[64,2,7,512]{3,1,2,0:T(2,128)} %all-to-all-done.1) | data formatting | bytes 3670016 | tf_op jit(solution)/shard_map/reshape | solution.py:183
  155.4 4.6 %scatter_fusion.1 = f32[33,7,512]{2,1,0:T(8,128)S(1)} fusion(f32[33,7,512]{2,1,0:T(8,128)S(1)} %broadcast_in_dim.16, s32[128]{0:T(128)S(1)} %fusion.118, f32[128,7,512]{2,1,0:T(8,128)S(1)} %bitcast.194), kind=kCustom, calls=%fused_computation.1 | custom fusion | bytes 5505536 | tf_op jit(solution)/shard_map/scatter | solution.py:193
  160.1 1.0 copy.160
  (190 shorter events, 23.5 us)
Async XLA Ops:
  2.5 24.8 %collective-permute-start = (f32[7,8,16,128]{3,2,1,0:T(8,128)S(1)}, f32[7,8,16,128]{3,2,1,0:T(8,128)S(1)}, u32[]{:S(2)}, u32[]{:S(2)}) collective-permute-start(f32[7,8,16,128]{3,2,1,0:T(8,128)S(1)} %constant_dynamic-update-slice_fusion), channel_id=1, source_target_pairs={{64,0},{128,64},{192,128},{65,1},{129,65},{193,129},{66,2},{130,66... | collective-permute-start | bytes 1376264 | tf_op jit(solution)/shard_map/ppermute | solution.py:26
  8.1 92.0 %all-to-all-start = ((f32[64,1,1]{2,1,0:T(1,128)}), f32[64,1,1]{2,1,0:T(1,128)}, u32[]{:S(2)}, u32[]{:S(2)}) async-start(f32[64,1,1]{2,1,0:T(1,128)} %copy.153), calls=%async_computation | async-start | bytes 65536 | tf_op jit(solution)/shard_map/all_to_all | solution.py:181
  27.6 9.5 %collective-permute-start.3 = (f32[7,8,1,128]{3,1,2,0:T(8,128)S(1)}, f32[7,8,1,128]{3,1,2,0:T(8,128)S(1)}, u32[]{:S(2)}, u32[]{:S(2)}) collective-permute-start(f32[7,8,1,128]{3,1,2,0:T(8,128)S(1)} %bitcast.226), channel_id=1, source_target_pairs={{8,0},{16,8},{24,16},{32,24},{40,32},{48,40},{56,48},{0,56},{9,1},... | collective-permute-start | bytes 86024 | tf_op jit(solution)/shard_map/ppermute | solution.py:18
  30.7 6.5 %collective-permute-start.4 = (f32[7,8,1,128]{3,1,2,0:T(8,128)S(1)}, f32[7,8,1,128]{3,1,2,0:T(8,128)S(1)}, u32[]{:S(2)}, u32[]{:S(2)}) collective-permute-start(f32[7,8,1,128]{3,1,2,0:T(8,128)S(1)} %bitcast.225), channel_id=1, source_target_pairs={{0,8},{8,16},{16,24},{24,32},{32,40},{40,48},{48,56},{56,0},{1,9},... | collective-permute-start | bytes 86024 | tf_op jit(solution)/shard_map/ppermute | solution.py:17
  31.3 15.5 %collective-permute-start.1 = (f32[7,1,16,128]{3,2,1,0:T(8,128)}, f32[7,1,16,128]{3,2,1,0:T(8,128)}, u32[]{:S(2)}, u32[]{:S(2)}) collective-permute-start(f32[7,1,16,128]{3,2,1,0:T(8,128)} %get-tuple-element.112), channel_id=1, source_target_pairs={{64,0},{128,64},{192,128},{65,1},{129,65},{193,129},{66,2},{130,66... | collective-permute-start | bytes 172040 | tf_op jit(solution)/shard_map/ppermute | solution.py:18
  33.2 13.6 %collective-permute-start.2 = (f32[7,1,16,128]{3,2,1,0:T(8,128)S(1)}, f32[7,1,16,128]{3,2,1,0:T(8,128)}, u32[]{:S(2)}, u32[]{:S(2)}) collective-permute-start(f32[7,1,16,128]{3,2,1,0:T(8,128)S(1)} %get-tuple-element.113), channel_id=1, source_target_pairs={{0,64},{64,128},{128,192},{1,65},{65,129},{129,193},{2,66},{66,130... | collective-permute-start | bytes 172040 | tf_op jit(solution)/shard_map/ppermute | solution.py:17
  38.0 3.2 %collective-permute-start.5 = (f32[7,8,18,1]{2,1,3,0:T(8,128)S(1)}, f32[7,8,18,1]{2,1,3,0:T(8,128)S(1)}, u32[]{:S(2)}, u32[]{:S(2)}) collective-permute-start(f32[7,8,18,1]{2,1,3,0:T(8,128)S(1)} %copy.139), channel_id=1, source_target_pairs={{1,0},{2,1},{3,2},{4,3},{5,4},{6,5},{7,6},{0,7},{9,8},{10,9},{11,1... | collective-permute-start | bytes 12104 | tf_op jit(solution)/shard_map/ppermute | solution.py:18
  40.8 4.5 %collective-permute-start.6 = (f32[7,8,18,1]{2,1,3,0:T(8,128)S(1)}, f32[7,8,18,1]{2,1,3,0:T(8,128)S(1)}, u32[]{:S(2)}, u32[]{:S(2)}) collective-permute-start(f32[7,8,18,1]{2,1,3,0:T(8,128)S(1)} %copy.141), channel_id=1, source_target_pairs={{0,1},{1,2},{2,3},{3,4},{4,5},{5,6},{6,7},{7,0},{8,9},{9,10},{10,1... | collective-permute-start | bytes 12104 | tf_op jit(solution)/shard_map/ppermute | solution.py:17
  46.5 1.2 copy-start.21
  46.5 1.2 copy-start.39
  46.5 1.2 copy-start.41
  46.5 1.2 copy-start.43
  46.5 1.2 copy-start.45
  46.6 1.2 copy-start.47
  46.6 1.2 copy-start.49
  50.4 6.3 %collective-permute-start.10 = (f32[7,8,1,128]{3,1,2,0:T(8,128)S(1)}, f32[7,8,1,128]{3,1,2,0:T(8,128)S(1)}, u32[]{:S(2)}, u32[]{:S(2)}) collective-permute-start(f32[7,8,1,128]{3,1,2,0:T(8,128)S(1)} %bitcast.228), channel_id=1, source_target_pairs={{0,8},{8,16},{16,24},{24,32},{32,40},{40,48},{48,56},{56,0},{1,9},... | collective-permute-start | bytes 86024 | tf_op jit(solution)/shard_map/ppermute | solution.py:17
  50.7 16.2 %collective-permute-start.7 = (f32[7,1,16,128]{3,2,1,0:T(8,128)S(1)}, f32[7,1,16,128]{3,2,1,0:T(8,128)S(1)}, u32[]{:S(2)}, u32[]{:S(2)}) collective-permute-start(f32[7,1,16,128]{3,2,1,0:T(8,128)S(1)} %fusion.115), channel_id=1, source_target_pairs={{64,0},{128,64},{192,128},{65,1},{129,65},{193,129},{66,2},{130,66... | collective-permute-start | bytes 172040 | tf_op jit(solution)/shard_map/ppermute | solution.py:18
  53.5 4.8 %collective-permute-start.9 = (f32[7,8,1,128]{3,1,2,0:T(8,128)S(1)}, f32[7,8,1,128]{3,1,2,0:T(8,128)S(1)}, u32[]{:S(2)}, u32[]{:S(2)}) collective-permute-start(f32[7,8,1,128]{3,1,2,0:T(8,128)S(1)} %bitcast.227), channel_id=1, source_target_pairs={{8,0},{16,8},{24,16},{32,24},{40,32},{48,40},{56,48},{0,56},{9,1},... | collective-permute-start | bytes 86024 | tf_op jit(solution)/shard_map/ppermute | solution.py:18
  59.1 2.2 %collective-permute-start.11 = (f32[7,8,18,1]{2,1,3,0:T(8,128)S(1)}, f32[7,8,18,1]{2,1,3,0:T(8,128)S(1)}, u32[]{:S(2)}, u32[]{:S(2)}) collective-permute-start(f32[7,8,18,1]{2,1,3,0:T(8,128)S(1)} %copy.149), channel_id=1, source_target_pairs={{1,0},{2,1},{3,2},{4,3},{5,4},{6,5},{7,6},{0,7},{9,8},{10,9},{11,1... | collective-permute-start | bytes 12104 | tf_op jit(solution)/shard_map/ppermute | solution.py:18
  60.8 4.5 %collective-permute-start.12 = (f32[7,8,18,1]{2,1,3,0:T(8,128)S(1)}, f32[7,8,18,1]{2,1,3,0:T(8,128)S(1)}, u32[]{:S(2)}, u32[]{:S(2)}) collective-permute-start(f32[7,8,18,1]{2,1,3,0:T(8,128)S(1)} %copy.151), channel_id=1, source_target_pairs={{0,1},{1,2},{2,3},{3,4},{4,5},{5,6},{6,7},{7,0},{8,9},{9,10},{10,1... | collective-permute-start | bytes 12104 | tf_op jit(solution)/shard_map/ppermute | solution.py:17
  66.8 6.2 %copy-start.22 = (f32[4,8]{1,0:T(4,128)S(1)}, f32[4,8]{1,0:T(4,128)}, u32[]{:S(2)}) copy-start(f32[4,8]{1,0:T(4,128)} %broadcast_multiply_fusion.2) | copy-start | bytes 388
  66.8 6.2 %copy-start.40 = (f32[4]{0:T(128)S(1)}, f32[4]{0:T(128)}, u32[]{:S(2)}) copy-start(f32[4]{0:T(128)} %get-tuple-element.24) | copy-start | bytes 52
  66.8 6.2 %copy-start.42 = (f32[4]{0:T(128)S(1)}, f32[4]{0:T(128)}, u32[]{:S(2)}) copy-start(f32[4]{0:T(128)} %get-tuple-element.25) | copy-start | bytes 52
  66.8 6.2 %copy-start.44 = (f32[4]{0:T(128)S(1)}, f32[4]{0:T(128)}, u32[]{:S(2)}) copy-start(f32[4]{0:T(128)} %get-tuple-element.26) | copy-start | bytes 52
  66.9 6.2 %copy-start.46 = (f32[4]{0:T(128)S(1)}, f32[4]{0:T(128)}, u32[]{:S(2)}) copy-start(f32[4]{0:T(128)} %get-tuple-element.143) | copy-start | bytes 52
  66.9 6.2 %copy-start.48 = (f32[4]{0:T(128)S(1)}, f32[4]{0:T(128)}, u32[]{:S(2)}) copy-start(f32[4]{0:T(128)} %get-tuple-element.144) | copy-start | bytes 52
  66.9 6.2 %copy-start.50 = (f32[4]{0:T(128)S(1)}, f32[4]{0:T(128)}, u32[]{:S(2)}) copy-start(f32[4]{0:T(128)} %get-tuple-element.145) | copy-start | bytes 52
  66.9 6.2 %copy-start.52 = (f32[4]{0:T(128)S(1)}, f32[4]{0:T(128)}, u32[]{:S(2)}) copy-start(f32[4]{0:T(128)} %param.20) | copy-start | bytes 52
  66.9 6.1 %collective-permute-start.8 = (f32[7,1,16,128]{3,2,1,0:T(8,128)S(1)}, f32[7,1,16,128]{3,2,1,0:T(8,128)S(1)}, u32[]{:S(2)}, u32[]{:S(2)}) collective-permute-start(f32[7,1,16,128]{3,2,1,0:T(8,128)S(1)} %get-tuple-element.32), channel_id=1, source_target_pairs={{0,64},{64,128},{128,192},{1,65},{65,129},{129,193},{2,66},{66,130... | collective-permute-start | bytes 172040 | tf_op jit(solution)/shard_map/ppermute | solution.py:17
  74.9 1.9 %copy-start = (f32[4,8,16,128]{3,2,1,0:T(8,128)}, f32[4,8,16,128]{3,2,1,0:T(8,128)S(1)}, u32[]{:S(2)}) copy-start(f32[4,8,16,128]{3,2,1,0:T(8,128)S(1)} %get-tuple-element.27) | copy-start | bytes 786436
  76.7 5.9 %copy-start.1 = (f32[3,8,16,128]{3,2,1,0:T(8,128)}, f32[3,8,16,128]{3,2,1,0:T(8,128)S(1)}, u32[]{:S(2)}) copy-start(f32[3,8,16,128]{3,2,1,0:T(8,128)S(1)} %fusion.37) | copy-start | bytes 589828
  100.1 53.3 %all-to-all-start.1 = ((f32[64,2,7,512]{3,1,2,0:T(2,128)}), f32[64,2,7,512]{3,1,2,0:T(2,128)}, u32[]{:S(2)}, u32[]{:S(2)}) async-start(f32[64,2,7,512]{3,1,2,0:T(2,128)} %copy.157), calls=%async_computation.1 | async-start | bytes 3670016 | tf_op jit(solution)/shard_map/all_to_all | solution.py:174
  (37 other events, 36.1 us)
where the time goes:
time: 163 us; the launch traced here: 161 us
  waiting for transfers between devices  51.8 us (32%)
  local copies, waits for them, and re-layouts  43.7 us (27%)
  starting transfers between devices  42.8 us (26%)
  other arithmetic  20.4 us (13%)
  between operations  2.35 us (1%)
    all_to_all x1, waiting for transfers between devices, per_device(): lax.all_to_all(outgoing.reshape(owners, capacity, components, cube), ('gx...  42.4 us
    ppermute x6, starting transfers between devices, padded(): after = lax.ppermute(first, axis, down)  12.6 us
    all_to_all x1, starting transfers between devices, per_device(): lax.all_to_all(counts, ('gx', 'gy'), split_axis=0, concat_axis=0, tiled=T...  10.5 us
    ppermute x6, waiting for transfers between devices, padded(): before = lax.ppermute(last, axis, up)  8.17 us
    ppermute x6, starting transfers between devices, padded(): before = lax.ppermute(last, axis, up)  7.98 us
    transpose x1, local copies, waits for them, and re-layouts, per_device(): tiles.transpose(1, 3, 5, 0, 2, 4, 6).reshape(tile_count, components, cube)  7.91 us
    all_to_all x1, starting transfers between devices, per_device(): lax.all_to_all(outgoing.reshape(owners, capacity, components, cube), ('gx...  7.64 us
    reshape x1, local copies, waits for them, and re-layouts, per_device(): tiles = fields.reshape(components, tiles_z, TS, tiles_x, TS, tiles_y, TS)  5.81 us
  transfers between devices with their start and end apart: 15, of which 6 were waited for; matrix products, arithmetic and copies ran while one was open for 32% of the time, Pallas kernels for 0%

commit v1 on v0

v1 whole, which is shorter than its diff:
```python
import jax
import jax.numpy as jnp
from jax import lax
from jax.experimental import pallas as pl
from jax.experimental.pallas import tpu as pltpu
from jax.sharding import PartitionSpec as P

CZ, CX, CY = 8, 16, 128
KEPT = 6
WINDOW = CZ + 4
ROWS = CZ * CX
X_ROWS = 18
MARKER = 3.0e38
LIMIT = 1.0e30
F32 = jnp.float32

VMEM = pl.BlockSpec(memory_space=pltpu.VMEM)
SMEM = pl.BlockSpec(memory_space=pltpu.SMEM)


def lanes_of(rows):
    return lax.broadcasted_iota(jnp.int32, (rows, 128), 1)


def sublanes_of(rows):
    return lax.broadcasted_iota(jnp.int32, (rows, 128), 0)


def flag_row(flags_ref, b):
    group = lanes_of(8) // 8
    row = jnp.zeros((8, 128), F32)
    for d in range(16):
        row = jnp.where(group == d, flags_ref[0, 0, 0, b * 16 + d].astype(F32), row)
    return row


def kept(phases_ref, solutes_ref, c, z):
    return phases_ref[c, z] if c < 3 else solutes_ref[c - 3, z]


def pack_z(phases_ref, solutes_ref, flags_ref, down_ref, down2_ref, up_ref):
    flags = [flag_row(flags_ref, b) for b in range(2)]
    for c in range(KEPT):
        for z in range(CZ):
            plane = kept(phases_ref, solutes_ref, c, z)
            down_ref[c * CZ + z] = plane
            if z < 2:
                down2_ref[c * 2 + z] = plane
            if z == CZ - 1:
                up_ref[c] = plane
    for b in range(2):
        down_ref[KEPT * CZ, b * 8 : b * 8 + 8] = flags[b]
        up_ref[KEPT, b * 8 : b * 8 + 8] = flags[b]


def frame(
    phases_ref, solutes_ref, above_ref, above2_ref, below_ref, flags_ref, melt_ref, shift_ref, slab_ref,
    window_ref, low_ref, high_ref, raw_ref,
):
    slab = slab_ref[0]
    shift = shift_ref[0]
    at_bottom = slab == 0
    at_top = slab == 3
    for c in range(KEPT):
        fresh = jnp.full((CX, 128), 0.0 if c < 3 else melt_ref[c - 3], F32)
        raw_ref[c, 0:CX] = below_ref[c]
        for z in range(CZ):
            raw_ref[c, (1 + z) * CX : (2 + z) * CX] = kept(phases_ref, solutes_ref, c, z)
            raw_ref[c, (9 + z) * CX : (10 + z) * CX] = jnp.where(at_top, fresh, above_ref[c * CZ + z])
        for z in range(2):
            raw_ref[c, (17 + z) * CX : (18 + z) * CX] = jnp.where(slab >= 2, fresh, above2_ref[c * 2 + z])
        for w in range(WINDOW):
            start = pl.multiple_of((shift - 1 + w) * CX, CX)
            window_ref[c, w * CX : (w + 1) * CX] = raw_ref[c, pl.ds(start, CX)]

        @pl.when(at_bottom)
        def _(c=c):
            window_ref[c, CX : 2 * CX] = window_ref[c, 2 * CX : 3 * CX]

        @pl.when(at_top)
        def _(c=c):
            window_ref[c, 10 * CX : 11 * CX] = window_ref[c, 9 * CX : 10 * CX]

        for ref, near, far in ((low_ref, 0, 1), (high_ref, 15, 14)):
            ref[c * X_ROWS : c * X_ROWS + 8] = window_ref[c, pl.ds(CX + near, 8, stride=CX)]
            ref[c * X_ROWS + 8 : c * X_ROWS + 10] = window_ref[c, pl.ds(9 * CX + near, 2, stride=CX)]
            ref[c * X_ROWS + 10 : c * X_ROWS + 18] = window_ref[c, pl.ds(2 * CX + far, 8, stride=CX)]
    low_ref[KEPT * X_ROWS : KEPT * X_ROWS + 4] = flag_row(flags_ref, 0)[:4]
    high_ref[KEPT * X_ROWS : KEPT * X_ROWS + 4] = flag_row(flags_ref, 1)[:4]


def pack_y(window_ref, before_ref, after_ref, flags_ref, out_ref, inner_ref, ends_ref, sides_ref):
    def gather(rows, value_of):
        lane = lanes_of(rows)
        packed = jnp.zeros((rows, 128), F32)
        for c in range(KEPT):
            moved = pltpu.roll(value_of(c), 2 + 4 * c, 1)
            packed = jnp.where((lane >= 4 * c) & (lane < 4 * c + 4), moved, packed)
        return packed

    flags = jnp.concatenate([flag_row(flags_ref, b) for b in range(2)], axis=0)
    flags = pltpu.roll(flags, 25, 1)
    flag_lane = (lanes_of(CX) == 24) | (lanes_of(CX) == 25)
    for z in range(CZ):
        packed = gather(CX, lambda c: window_ref[c, (z + 2) * CX : (z + 3) * CX])
        inner_ref[z * CX : (z + 1) * CX] = jnp.where(flag_lane, flags, packed)
    ends_ref[...] = jnp.zeros((128, 128), F32)
    ends_ref[0:CX] = gather(CX, lambda c: window_ref[c, CX : 2 * CX])
    ends_ref[112:128] = gather(CX, lambda c: window_ref[c, 10 * CX : 11 * CX])
    sides_ref[...] = jnp.zeros((128, 128), F32)
    sides_ref[pl.ds(0, 8, stride=CX)] = gather(8, lambda c: before_ref[c * X_ROWS + 1 : c * X_ROWS + 9])
    sides_ref[pl.ds(15, 8, stride=CX)] = gather(8, lambda c: after_ref[c * X_ROWS + 1 : c * X_ROWS + 9])
    out_ref[0:32] = inner_ref[...].T[0:32]
    out_ref[32:56] = ends_ref[...].T[0:24]
    out_ref[56:80] = sides_ref[...].T[0:24]


def read_parameters(stiffness_ref, barrier_ref, coupling_ref, slope_ref, diffusivity_ref, release_ref):
    return dict(
        stiffness=[[stiffness_ref[a, e] for e in range(3)] for a in range(4)],
        barrier=[barrier_ref[a] for a in range(4)],
        coupling=[[coupling_ref[a, k] for k in range(3)] for a in range(4)],
        slope=[slope_ref[a] for a in range(4)],
        base=[0.5 * diffusivity_ref[3, k] for k in range(3)],
        excess=[[0.5 * (diffusivity_ref[a, k] - diffusivity_ref[3, k]) for k in range(3)] for a in range(3)],
        release=[[release_ref[a, k] for k in range(3)] for a in range(4)],
    )


def advance(own, neighbours, flag, height, par):
    fractions = list(own[:3])
    fractions.append(1.0 - (own[0] + own[1] + own[2]))
    solutes = own[3:]

    def half_density(at, k):
        return par["base"][k] + (
            par["excess"][0][k] * at[0] + par["excess"][1][k] * at[1] + par["excess"][2][k] * at[2]
        )

    own_density = [half_density(own, k) for k in range(3)]
    gains = [None] * 3
    laplace = [None] * 4
    for e, (upper, lower) in enumerate(neighbours):
        curve = [upper[a] + lower[a] - 2.0 * own[a] for a in range(3)]
        curve.append(-(curve[0] + curve[1] + curve[2]))
        for a in range(4):
            term = par["stiffness"][a][e] * curve[a]
            laplace[a] = term if laplace[a] is None else laplace[a] + term
        for beside in (upper, lower):
            for k in range(3):
                flow = (own_density[k] + half_density(beside, k)) * (beside[3 + k] - solutes[k])
                gains[k] = flow if gains[k] is None else gains[k] + flow
    rates = []
    for a in range(4):
        p = fractions[a]
        drive = par["slope"][a] * height + par["barrier"][a] * (2.0 * p - 1.0)
        for k in range(3):
            drive = drive + par["coupling"][a][k] * solutes[k]
        rates.append(flag * (laplace[a] + p * (1.0 - p) * drive))
    mean = 0.25 * (rates[0] + rates[1] + rates[2] + rates[3])
    changes = [rate - mean for rate in rates]
    after = [fractions[a] + changes[a] for a in range(4)]
    for k in range(3):
        released = par["release"][0][k] * changes[0]
        for a in range(1, 4):
            released = released + par["release"][a][k] * changes[a]
        after.append(solutes[k] + gains[k] + released)
    return after[:3] + after[4:], after[3]


def steps(
    window_ref, before_ref, after_ref, own_y_ref, left_ref, right_ref, above_ref, below_ref,
    flags_ref, slots_ref, slab_ref,
    stiffness_ref, barrier_ref, coupling_ref, slope_ref, diffusivity_ref, release_ref,
    phases_ref, solutes_ref, send_ref,
    edge_ref, turned_ref, first_ref, xface_ref, final_ref,
):
    slab = slab_ref[0]
    at_bottom = slab == 0
    at_top = slab == 3
    par = read_parameters(stiffness_ref, barrier_ref, coupling_ref, slope_ref, diffusivity_ref, release_ref)
    first_row = (slab * CZ).astype(F32)

    def height_of(z):
        return (first_row + z + 0.5) / 32.0 - 0.5

    lane16, lane8, sub16 = lanes_of(CX), lanes_of(8), sublanes_of(CX)
    flags = jnp.concatenate([flag_row(flags_ref, b) for b in range(2)], axis=0)

    edge_ref[...] = jnp.zeros((128, 128), F32)
    for group, start in ((0, 0), (1, 32), (2, 56)):
        for c in range(KEPT):
            at = group * 12 + 2 * c
            edge_ref[at : at + 1] = right_ref[start + 4 * c + 2 : start + 4 * c + 3]
            edge_ref[at + 1 : at + 2] = left_ref[start + 4 * c + 1 : start + 4 * c + 2]
    turned_ref[...] = edge_ref[...].T

    def beside_y(value, rows, column):
        lane = lane16 if value.shape[0] == CX else lane8
        fill = pltpu.roll(rows, 127 - column, 1)
        upper = jnp.where(lane == 127, fill, pltpu.roll(value, 127, 1))
        lower = jnp.where(lane == 0, fill, pltpu.roll(value, 1, 1))
        return upper, lower

    def beside_x(ref, c, start, low_row, high_row):
        upper = jnp.where(sub16 == 15, high_row, ref[c, start + 1 : start + 1 + CX])
        lower = jnp.where(sub16 == 0, low_row, ref[c, start - 1 : start - 1 + CX])
        return upper, lower

    def split(pairs):
        return ([pair[0] for pair in pairs], [pair[1] for pair in pairs])

    for w in range(1, WINDOW - 1):
        z = w - 2
        start = w * CX
        own = [window_ref[c, start : start + CX] for c in range(KEPT)]
        along_z = (
            [window_ref[c, start + CX : start + 2 * CX] for c in range(KEPT)],
            [window_ref[c, start - CX : start] for c in range(KEPT)],
        )
        along_x = split(
            [
                beside_x(
                    window_ref, c, start,
                    before_ref[c * X_ROWS + z + 1 : c * X_ROWS + z + 2],
                    after_ref[c * X_ROWS + z + 1 : c * X_ROWS + z + 2],
                )
                for c in range(KEPT)
            ]
        )
        if z == -1:
            rows, group, flag = turned_ref[0:CX], 1, below_ref[KEPT]
        elif z == CZ:
            rows, group, flag = turned_ref[112:128], 1, above_ref[KEPT * CZ]
        else:
            rows, group, flag = turned_ref[z * CX : (z + 1) * CX], 0, flags
        along_y = split([beside_y(own[c], rows, group * 12 + 2 * c) for c in range(KEPT)])
        result, _ = advance(own, (along_z, along_x, along_y), flag, height_of(z), par)
        for c in range(KEPT):
            first_ref[c, (w - 1) * CX : w * CX] = result[c]

    @pl.when(at_bottom)
    def _():
        for c in range(KEPT):
            first_ref[c, 0:CX] = first_ref[c, CX : 2 * CX]

    @pl.when(at_top)
    def _():
        for c in range(KEPT):
            first_ref[c, 9 * CX : 10 * CX] = first_ref[c, 8 * CX : 9 * CX]

    face_height = height_of(sublanes_of(8).astype(F32))
    for side, ref, x in ((0, before_ref, 0), (1, after_ref, 15)):
        own = [ref[c * X_ROWS + 1 : c * X_ROWS + 9] for c in range(KEPT)]
        along_z = (
            [ref[c * X_ROWS + 2 : c * X_ROWS + 10] for c in range(KEPT)],
            [ref[c * X_ROWS : c * X_ROWS + 8] for c in range(KEPT)],
        )
        along_x = (
            [ref[c * X_ROWS + 10 : c * X_ROWS + 18] for c in range(KEPT)],
            [window_ref[c, pl.ds(2 * CX + x, 8, stride=CX)] for c in range(KEPT)],
        )
        rows = turned_ref[pl.ds(x, 8, stride=CX)]
        along_y = split([beside_y(own[c], rows, 24 + 2 * c) for c in range(KEPT)])
        flag = ref[KEPT * X_ROWS : KEPT * X_ROWS + 1]
        result, _ = advance(own, (along_z, along_x, along_y), flag, face_height, par)
        for c in range(KEPT):
            xface_ref[side * KEPT + c] = result[c]

    sub8 = sublanes_of(8)

    def both(right_row, left_row):
        return jnp.where(sub8 == 0, right_row, left_row)

    def lifted(c, start):
        return both(
            right_ref[start + 4 * c + 2 : start + 4 * c + 3],
            left_ref[start + 4 * c + 1 : start + 4 * c + 2],
        )

    own = [lifted(c, 0) for c in range(KEPT)]
    ends = [lifted(c, 32) for c in range(KEPT)]
    sides = [lifted(c, 56) for c in range(KEPT)]
    outer = [both(right_ref[4 * c + 3 : 4 * c + 4], left_ref[4 * c : 4 * c + 1]) for c in range(KEPT)]
    inner = [both(own_y_ref[4 * c + 1 : 4 * c + 2], own_y_ref[4 * c + 2 : 4 * c + 3]) for c in range(KEPT)]
    along_z = (
        [jnp.where(lane8 >= 112, ends[c], pltpu.roll(own[c], 112, 1)) for c in range(KEPT)],
        [jnp.where(lane8 < 16, ends[c], pltpu.roll(own[c], 16, 1)) for c in range(KEPT)],
    )
    along_x = (
        [jnp.where(lane8 % 16 == 15, sides[c], pltpu.roll(own[c], 127, 1)) for c in range(KEPT)],
        [jnp.where(lane8 % 16 == 0, sides[c], pltpu.roll(own[c], 1, 1)) for c in range(KEPT)],
    )
    flag = both(right_ref[25:26], left_ref[24:25])
    result, _ = advance(
        own, (along_z, along_x, (outer, inner)), flag, height_of((lane8 // 16).astype(F32)), par
    )
    for c in range(KEPT):
        edge_ref[2 * c : 2 * c + 2] = result[c][0:2]
    turned_ref[...] = edge_ref[...].T

    for z in range(CZ):
        start = (z + 1) * CX
        own = [first_ref[c, start : start + CX] for c in range(KEPT)]
        along_z = (
            [first_ref[c, start + CX : start + 2 * CX] for c in range(KEPT)],
            [first_ref[c, start - CX : start] for c in range(KEPT)],
        )
        along_x = split(
            [
                beside_x(first_ref, c, start, xface_ref[c, z : z + 1], xface_ref[KEPT + c, z : z + 1])
                for c in range(KEPT)
            ]
        )
        rows = turned_ref[z * CX : (z + 1) * CX]
        along_y = split([beside_y(own[c], rows, 2 * c) for c in range(KEPT)])
        result, last = advance(own, (along_z, along_x, along_y), flags, height_of(z), par)
        for c in range(3):
            phases_ref[c, z] = result[c]
            solutes_ref[c, z] = result[3 + c]
        phases_ref[3, z] = last
        for c in range(KEPT):
            final_ref[c * ROWS + z * CX : c * ROWS + (z + 1) * CX] = result[c]

    for owner in range(64):
        send_ref[2 * owner, 0:1] = jnp.full((1, 128), MARKER, F32)
    group = lane8 // 8
    for b in range(2):
        for q in range(4):
            parts = []
            for i in range(16):
                row = (2 * q + i // 8) * CX + b * 8 + i % 8
                parts.append(final_ref[pl.ds(row, 8, stride=ROWS)])
            for step in (8, 4, 2, 1):
                keep = (group & step) == 0
                swapped = list(parts)
                for i in range(16):
                    if i & step == 0:
                        one, two = parts[i], parts[i + step]
                        swapped[i] = jnp.where(keep, one, pltpu.roll(two, step * 8, 1))
                        swapped[i + step] = jnp.where(keep, pltpu.roll(one, 128 - step * 8, 1), two)
                parts = swapped
            for d in range(16):
                send_ref[slots_ref[b * 16 + d], 6 * q : 6 * q + 6] = parts[d][0:6]


def place(arrived_ref, moved_ref):
    sub16 = sublanes_of(16)
    weight = jnp.zeros((16, 128), F32)
    for i in range(16):
        weight = jnp.where((sub16 == i) & (lanes_of(16) == 0), float(2**i), weight)
    masks = []
    for block in range(4):
        first = jnp.concatenate([arrived_ref[2 * (block * 16 + i), 0:1] for i in range(16)], axis=0)
        masks.append(jnp.sum(jnp.where(first < LIMIT, weight, 0.0)).astype(jnp.int32))
    count = jnp.int32(0)
    for block in range(4):

        def one_source(i, count, block=block):
            present = (masks[block] >> i) & 1
            source = block * 16 + i

            @pl.when((present == 1) & (count < 31))
            def _():
                for e in range(2):
                    for q in range(4):
                        part = arrived_ref[2 * source + e, 6 * q : 6 * q + 6]
                        span = slice(q * 128, (q + 1) * 128)
                        moved_ref[count + e, 0:3, span] = part[0:3]
                        moved_ref[count + e, 3:4, span] = 1.0 - (part[0:1] + part[1:2] + part[2:3])
                        moved_ref[count + e, 4:7, span] = part[3:6]

            return count + 2 * present

        count = lax.fori_loop(0, 16, one_source, count)


def shape_of(*dims):
    return jax.ShapeDtypeStruct(dims, F32)


PARAMS = pltpu.CompilerParams(vmem_limit_bytes=32 * 1024 * 1024)


def call(body, ins, outs, scratch=(), flops=0):
    return pl.pallas_call(
        body,
        in_specs=list(ins),
        out_specs=[VMEM] * len(outs),
        out_shape=list(outs),
        scratch_shapes=list(scratch),
        compiler_params=PARAMS,
        cost_estimate=pl.CostEstimate(flops=flops, bytes_accessed=1000000, transcendentals=0),
    )


def shifted(value, axis, by, wrap):
    count = lax.axis_size(axis)
    pairs = [
        (source, (source + by) % count) for source in range(count) if wrap or 0 <= source + by < count
    ]
    return lax.ppermute(value, axis, pairs)


def per_device(
    phases, solutes, melt, shift_rows, flags, balance,
    stiffness, barrier, coupling, slope, diffusivity, release,
):
    slab = lax.axis_index("gz").astype(jnp.int32).reshape(1)
    owner_list = balance.reshape(32)
    serial = jnp.arange(32)
    earlier = jnp.sum(
        ((owner_list[:, None] == owner_list[None, :]) & (serial[None, :] < serial[:, None])).astype(jnp.int32),
        axis=1,
    )
    slots = owner_list * 2 + earlier

    down, down2, up = call(
        pack_z,
        [VMEM, VMEM, SMEM],
        [shape_of(KEPT * CZ + 1, CX, 128), shape_of(KEPT * 2, CX, 128), shape_of(KEPT + 1, CX, 128)],
    )(phases, solutes, flags)
    above = shifted(down, "gz", -1, False)
    above2 = shifted(down2, "gz", -2, False)
    below = shifted(up, "gz", 1, False)

    window, low, high = call(
        frame,
        [VMEM] * 5 + [SMEM] * 4,
        [shape_of(KEPT, WINDOW * CX, 128), shape_of(112, 128), shape_of(112, 128)],
        [pltpu.VMEM((KEPT, 19 * CX, 128), F32)],
    )(phases, solutes, above, above2, below, flags, melt, shift_rows, slab)
    before = shifted(high, "gx", 1, True)
    after = shifted(low, "gx", -1, True)

    (faces,) = call(
        pack_y,
        [VMEM] * 3 + [SMEM],
        [shape_of(80, 128)],
        [pltpu.VMEM((128, 128), F32)] * 3,
    )(window, before, after, flags)
    left = shifted(faces, "gy", 1, True)
    right = shifted(faces, "gy", -1, True)

    phases_out, solutes_out, send = call(
        steps,
        [VMEM] * 8 + [SMEM] * 9,
        [shape_of(4, CZ, CX, CY), shape_of(3, CZ, CX, CY), shape_of(128, 24, 128)],
        [
            pltpu.VMEM((128, 128), F32),
            pltpu.VMEM((128, 128), F32),
            pltpu.VMEM((KEPT, 10 * CX, 128), F32),
            pltpu.VMEM((2 * KEPT, 8, 128), F32),
            pltpu.VMEM((8 * ROWS, 128), F32),
        ],
    )(
        window, before, after, faces, left, right, above, below, flags, slots, slab,
        stiffness, barrier, coupling, slope, diffusivity, release,
    )
    arrived = lax.all_to_all(send, ("gx", "gy"), split_axis=0, concat_axis=0, tiled=True)
    (moved,) = call(place, [VMEM], [shape_of(32, 7, 512)])(arrived)
    return phases_out, solutes_out, moved


def solution(mesh):
    block = P(None, "gz", "gx", "gy")
    table = P("gz", "gx", "gy", None)
    return jax.shard_map(
        per_device,
        mesh=mesh,
        in_specs=(block, block, P(), P(), table, table, P(), P(), P(), P(), P(), P()),
        out_specs=(block, block, P(("gz", "gx", "gy"), None, None)),
        check_vma=False,
    )
```

time: 163 us -> 93.6 us (0.57)
  blocking collectives: 0 us -> 48.4 us
  waiting for transfers between devices: 51.8 us -> 12.1 us
  local copies, waits for them, and re-layouts: 43.7 us -> 6.78 us
  starting transfers between devices: 42.8 us -> 15.3 us
  other arithmetic: 20.4 us -> 0.91 us
  Pallas kernels: 0 us -> 8.42 us
    all_to_all x0 -> x1, blocking collectives: none -> 48.4 us  [per_device(): lax.all_to_all(send, ('gx', 'gy'), split_axis=0, concat_axis=0, tiled=True)]
    all_to_all x2 -> x0, waiting for transfers between devices: 42.4 us -> none  [the longest x1 42.4 us: per_device(): lax.all_to_all(outgoing.reshape(owners, capacity, components, cube), ('gx...]
    all_to_all x2 -> x0, starting transfers between devices: 18.1 us -> none  [the longest x1 10.5 us: per_device(): lax.all_to_all(counts, ('gx', 'gy'), split_axis=0, concat_axis=0, tiled=T...]
    reshape x5 -> x0, local copies, waits for them, and re-layouts: 15.2 us -> none  [the longest x1 5.81 us: per_device(): tiles = fields.reshape(components, tiles_z, TS, tiles_x, TS, tiles_y, TS)]
    ppermute x13 -> x7, starting transfers between devices: 24.7 us -> 15.3 us  [shifted(): return lax.ppermute(value, axis, pairs)]
    pallas_call x0 -> x5, Pallas kernels: none -> 8.42 us  [the longest x1 5.21 us: per_device(): call(steps, [VMEM] * 8 + [SMEM] * 9, [shape_of(4, CZ, CX, CY), shape_of(3...]
    transpose x1 -> x0, local copies, waits for them, and re-layouts: 7.91 us -> none  [per_device(): tiles.transpose(1, 3, 5, 0, 2, 4, 6).reshape(tile_count, components, cube)]
    scatter x2 -> x0, local copies, waits for them, and re-layouts: 6.16 us -> none  [the longest x1 4.65 us: per_device(): moved = jnp.zeros((tile_count + 1, components, cube), fields.dtype).at[pl...]
  transfers between devices with their start and end apart: 15 -> 7, of which waited for: 6 -> 5; matrix products, arithmetic and copies ran while one was open for 32% -> 1% of each run, Pallas kernels for 0% -> 0%
where the time goes in v1:
time: 93.6 us; the launch traced here: 93.3 us
  blocking collectives  48.4 us (52%)
  starting transfers between devices  15.3 us (16%)
  waiting for transfers between devices  12.1 us (13%)
  Pallas kernels  8.42 us (9%)
  local copies, waits for them, and re-layouts  6.78 us (7%)
  between operations  1.41 us (2%)
    all_to_all x1, blocking collectives, per_device(): lax.all_to_all(send, ('gx', 'gy'), split_axis=0, concat_axis=0, tiled=True)  48.4 us
    ppermute x7, starting transfers between devices, shifted(): return lax.ppermute(value, axis, pairs)  15.3 us
    ppermute x7, waiting for transfers between devices, shifted(): return lax.ppermute(value, axis, pairs)  12.1 us
    unnamed x29, local copies, waits for them, and re-layouts  6.78 us
    pallas_call x1, Pallas kernels, per_device(): call(steps, [VMEM] * 8 + [SMEM] * 9, [shape_of(4, CZ, CX, CY), shape_of(3...  5.21 us
  transfers between devices with their start and end apart: 7, of which 5 were waited for; matrix products, arithmetic and copies ran while one was open for 1% of the time, Pallas kernels for 0%

profile of v1, /device:TPU:8, one launch (start us, length us, event | category | flops | bytes accessed | tf_op | source)
XLA Modules:
  0.0 93.3 jit_solution(16457742175702776571)
XLA Ops:
  0.6 0.0 copy-start
  0.6 0.9 %copy-done = f32[4,8,16,128]{3,2,1,0:T(8,128)S(1)} copy-done((f32[4,8,16,128]{3,2,1,0:T(8,128)S(1)}, f32[4,8,16,128]{3,2,1,0:T(8,128)}, u32[]{:S(2)}) %copy-start) | copy-done | bytes 262168
  1.6 0.9 copy-done.2
  2.5 0.7 copy-done.4
  3.2 0.0 copy-start.9
  3.2 0.0 copy-start.11
  3.2 0.6 shard_map.139
  3.8 4.1 %collective-permute-start = (f32[49,16,128]{2,1,0:T(8,128)S(1)}, f32[49,16,128]{2,1,0:T(8,128)S(1)}, u32[]{:S(2)}, u32[]{:S(2)}) collective-permute-start(f32[49,16,128]{2,1,0:T(8,128)S(1)} %get-tuple-element.12), channel_id=1, source_target_pairs={{64,0},{128,64},{192,128},{65,1},{129,65},{193,129},{66,2},{130,66... | collective-permute-start | bytes 1204232 | tf_op jit(solution)/shard_map/ppermute | solution.py:402
  7.9 1.3 %collective-permute-start.1 = (f32[12,16,128]{2,1,0:T(8,128)S(1)}, f32[12,16,128]{2,1,0:T(8,128)S(1)}, u32[]{:S(2)}, u32[]{:S(2)}) collective-permute-start(f32[12,16,128]{2,1,0:T(8,128)S(1)} %get-tuple-element.13), channel_id=1, source_target_pairs={{128,0},{192,64},{129,1},{193,65},{130,2},{194,66},{131,3},{195,67... | collective-permute-start | bytes 294920 | tf_op jit(solution)/shard_map/ppermute | solution.py:402
  9.2 3.4 %collective-permute-start.2 = (f32[7,16,128]{2,1,0:T(8,128)S(1)}, f32[7,16,128]{2,1,0:T(8,128)S(1)}, u32[]{:S(2)}, u32[]{:S(2)}) collective-permute-start(f32[7,16,128]{2,1,0:T(8,128)S(1)} %get-tuple-element.14), channel_id=1, source_target_pairs={{0,64},{64,128},{128,192},{1,65},{65,129},{129,193},{2,66},{66,130... | collective-permute-start | bytes 172040 | tf_op jit(solution)/shard_map/ppermute | solution.py:402
  13.2 2.0 %collective-permute-done.2.below_ref = f32[7,16,128]{2,1,0:T(8,128)S(1)} collective-permute-done((f32[7,16,128]{2,1,0:T(8,128)S(1)}, f32[7,16,128]{2,1,0:T(8,128)S(1)}, u32[]{:S(2)}, u32[]{:S(2)}) %collective-permute-start.2) | collective-permute-done | bytes 57376 | tf_op jit(solution)/shard_map/ppermute | solution.py:402
  15.3 4.6 %collective-permute-done.1.above2_ref = f32[12,16,128]{2,1,0:T(8,128)S(1)} collective-permute-done((f32[12,16,128]{2,1,0:T(8,128)S(1)}, f32[12,16,128]{2,1,0:T(8,128)S(1)}, u32[]{:S(2)}, u32[]{:S(2)}) %collective-permute-start.1) | collective-permute-done | bytes 98336 | tf_op jit(solution)/shard_map/ppermute | solution.py:402
  19.8 0.0 collective-permute-done.above_ref
  19.8 0.9 %copy-done.1 = f32[4,8,16,128]{3,2,1,0:T(8,128)S(1)} copy-done((f32[4,8,16,128]{3,2,1,0:T(8,128)S(1)}, f32[4,8,16,128]{3,2,1,0:T(8,128)}, u32[]{:S(2)}) %copy-start.1) | copy-done | bytes 262168
  20.8 0.9 copy-done.3
  21.7 0.7 copy-done.5
  22.4 0.7 copy-done.10
  23.0 0.7 shard_map.140
  23.8 2.0 %collective-permute-start.3 = (f32[112,128]{1,0:T(8,128)S(1)}, f32[112,128]{1,0:T(8,128)S(1)}, u32[]{:S(2)}, u32[]{:S(2)}) collective-permute-start(f32[112,128]{1,0:T(8,128)S(1)} %get-tuple-element.16), channel_id=1, source_target_pairs={{0,8},{8,16},{16,24},{24,32},{32,40},{40,48},{48,56},{56,0},{1,9},... | collective-permute-start | bytes 172040 | tf_op jit(solution)/shard_map/ppermute | solution.py:402
  25.8 4.0 %collective-permute-start.4 = (f32[112,128]{1,0:T(8,128)S(1)}, f32[112,128]{1,0:T(8,128)S(1)}, u32[]{:S(2)}, u32[]{:S(2)}) collective-permute-start(f32[112,128]{1,0:T(8,128)S(1)} %get-tuple-element.17), channel_id=1, source_target_pairs={{0,56},{8,0},{16,8},{24,16},{32,24},{40,32},{48,40},{56,48},{1,57}... | collective-permute-start | bytes 172040 | tf_op jit(solution)/shard_map/ppermute | solution.py:402
  29.8 0.9 convert_reduce_fusion
  30.7 1.2 %collective-permute-done.3.before_ref = f32[112,128]{1,0:T(8,128)S(1)} collective-permute-done((f32[112,128]{1,0:T(8,128)S(1)}, f32[112,128]{1,0:T(8,128)S(1)}, u32[]{:S(2)}, u32[]{:S(2)}) %collective-permute-start.3) | collective-permute-done | bytes 57376 | tf_op jit(solution)/shard_map/ppermute | solution.py:402
  31.9 0.0 collective-permute-done.4.after_ref
  31.9 0.8 shard_map.141.own_y_ref
  32.7 0.2 collective-permute-start.6
  32.9 0.3 collective-permute-start.5
  33.2 1.3 %collective-permute-done.6.right_ref = f32[80,128]{1,0:T(8,128)S(1)} collective-permute-done((f32[80,128]{1,0:T(8,128)S(1)}, f32[80,128]{1,0:T(8,128)S(1)}, u32[]{:S(2)}, u32[]{:S(2)}) %collective-permute-start.6) | collective-permute-done | bytes 40992 | tf_op jit(solution)/shard_map/ppermute | solution.py:402
  34.5 3.0 %collective-permute-done.5.left_ref = f32[80,128]{1,0:T(8,128)S(1)} collective-permute-done((f32[80,128]{1,0:T(8,128)S(1)}, f32[80,128]{1,0:T(8,128)S(1)}, u32[]{:S(2)}, u32[]{:S(2)}) %collective-permute-start.5) | collective-permute-done | bytes 40992 | tf_op jit(solution)/shard_map/ppermute | solution.py:402
  37.5 5.2 %shard_map.142 = (f32[4,8,16,128]{3,2,1,0:T(8,128)}, f32[3,8,16,128]{3,2,1,0:T(8,128)}, f32[128,24,128]{2,1,0:T(8,128)S(1)}) custom-call(f32[6,192,128]{2,1,0:T(8,128)S(1)} %get-tuple-element.15.window_ref, f32[112,128]{1,0:T(8,128)S(1)} %collective-permute-done.3.before_ref, f32[112,128]{1,0:T(8,128)S(1)} %collective-permute-done.4.after_ref, ...), custom_call_target="tpu_custom_call" | custom-call | bytes 1000000 | tf_op jit(solution)/shard_map/pallas_call | solution.py:445
  42.8 48.4 %all_to_all.5.arrived_ref = f32[128,24,128]{2,1,0:T(8,128)S(1)} all-to-all(f32[128,24,128]{2,1,0:T(8,128)S(1)} %get-tuple-element.20), channel_id=1, replica_groups=mesh['gz'=4,'gx'=8,'gy'=8] {'gx','gy'}, dimensions={0} | all-to-all | bytes 3145728 | tf_op jit(solution)/shard_map/all_to_all | solution.py:460
  91.2 1.1 %shard_map.143 = f32[32,7,512]{2,1,0:T(8,128)S(1)} custom-call(f32[128,24,128]{2,1,0:T(8,128)S(1)} %all_to_all.5.arrived_ref), custom_call_target="tpu_custom_call" | custom-call | bytes 1000000 | tf_op jit(solution)/shard_map/pallas_call | solution.py:461
  92.3 1.0 %copy.16 = f32[32,7,512]{2,0,1:T(8,128)} copy(f32[32,7,512]{2,1,0:T(8,128)S(1)} %shard_map.143) | data formatting | bytes 917504
  (19 shorter events, 0.0 us)
Async XLA Ops:
  0.6 1.0 %copy-start = (f32[4,8,16,128]{3,2,1,0:T(8,128)S(1)}, f32[4,8,16,128]{3,2,1,0:T(8,128)}, u32[]{:S(2)}) copy-start(f32[4,8,16,128]{3,2,1,0:T(8,128)} %phases_ref.3) | copy-start | bytes 786436
  1.6 0.9 copy-start.2
  2.5 0.7 copy-start.4
  3.2 30.0 %copy-start.13 = (s32[1,1,1,32]{3,2,1,0:T(1,128)S(1)}, s32[1,1,1,32]{3,2,1,0:T(1,128)}, u32[]{:S(2)}) copy-start(s32[1,1,1,32]{3,2,1,0:T(1,128)} %param.17) | copy-start | bytes 388
  3.2 34.3 %copy-start.6 = (f32[4,3]{1,0:T(4,128)S(1)}, f32[4,3]{1,0:T(4,128)}, u32[]{:S(2)}) copy-start(f32[4,3]{1,0:T(4,128)} %stiffness_ref.1) | copy-start | bytes 148
  3.2 34.3 %copy-start.7 = (f32[4,3]{1,0:T(4,128)S(1)}, f32[4,3]{1,0:T(4,128)}, u32[]{:S(2)}) copy-start(f32[4,3]{1,0:T(4,128)} %coupling_ref.1) | copy-start | bytes 148
  3.2 34.3 %copy-start.8 = (f32[4,3]{1,0:T(4,128)S(1)}, f32[4,3]{1,0:T(4,128)}, u32[]{:S(2)}) copy-start(f32[4,3]{1,0:T(4,128)} %diffusivity_ref.1) | copy-start | bytes 148
  3.2 34.3 %copy-start.9 = (f32[4,3]{1,0:T(4,128)S(1)}, f32[4,3]{1,0:T(4,128)}, u32[]{:S(2)}) copy-start(f32[4,3]{1,0:T(4,128)} %release_ref.1) | copy-start | bytes 148
  3.2 34.3 %copy-start.11 = (f32[4]{0:T(128)S(1)}, f32[4]{0:T(128)}, u32[]{:S(2)}) copy-start(f32[4]{0:T(128)} %barrier_ref.1) | copy-start | bytes 52
  3.2 34.3 %copy-start.12 = (f32[4]{0:T(128)S(1)}, f32[4]{0:T(128)}, u32[]{:S(2)}) copy-start(f32[4]{0:T(128)} %slope_ref.1) | copy-start | bytes 52
  3.8 16.0 %collective-permute-start = (f32[49,16,128]{2,1,0:T(8,128)S(1)}, f32[49,16,128]{2,1,0:T(8,128)S(1)}, u32[]{:S(2)}, u32[]{:S(2)}) collective-permute-start(f32[49,16,128]{2,1,0:T(8,128)S(1)} %get-tuple-element.12), channel_id=1, source_target_pairs={{64,0},{128,64},{192,128},{65,1},{129,65},{193,129},{66,2},{130,66... | collective-permute-start | bytes 1204232 | tf_op jit(solution)/shard_map/ppermute | solution.py:402
  7.9 11.9 %collective-permute-start.1 = (f32[12,16,128]{2,1,0:T(8,128)S(1)}, f32[12,16,128]{2,1,0:T(8,128)S(1)}, u32[]{:S(2)}, u32[]{:S(2)}) collective-permute-start(f32[12,16,128]{2,1,0:T(8,128)S(1)} %get-tuple-element.13), channel_id=1, source_target_pairs={{128,0},{192,64},{129,1},{193,65},{130,2},{194,66},{131,3},{195,67... | collective-permute-start | bytes 294920 | tf_op jit(solution)/shard_map/ppermute | solution.py:402
  9.2 6.1 %collective-permute-start.2 = (f32[7,16,128]{2,1,0:T(8,128)S(1)}, f32[7,16,128]{2,1,0:T(8,128)S(1)}, u32[]{:S(2)}, u32[]{:S(2)}) collective-permute-start(f32[7,16,128]{2,1,0:T(8,128)S(1)} %get-tuple-element.14), channel_id=1, source_target_pairs={{0,64},{64,128},{128,192},{1,65},{65,129},{129,193},{2,66},{66,130... | collective-permute-start | bytes 172040 | tf_op jit(solution)/shard_map/ppermute | solution.py:402
  19.8 1.0 %copy-start.1 = (f32[4,8,16,128]{3,2,1,0:T(8,128)S(1)}, f32[4,8,16,128]{3,2,1,0:T(8,128)}, u32[]{:S(2)}) copy-start(f32[4,8,16,128]{3,2,1,0:T(8,128)} %phases_ref.3) | copy-start | bytes 786436
  20.8 0.9 copy-start.3
  21.7 0.7 copy-start.5
  22.4 0.7 copy-start.10
  23.8 8.1 %collective-permute-start.3 = (f32[112,128]{1,0:T(8,128)S(1)}, f32[112,128]{1,0:T(8,128)S(1)}, u32[]{:S(2)}, u32[]{:S(2)}) collective-permute-start(f32[112,128]{1,0:T(8,128)S(1)} %get-tuple-element.16), channel_id=1, source_target_pairs={{0,8},{8,16},{16,24},{24,32},{32,40},{40,48},{48,56},{56,0},{1,9},... | collective-permute-start | bytes 172040 | tf_op jit(solution)/shard_map/ppermute | solution.py:402
  25.8 6.1 %collective-permute-start.4 = (f32[112,128]{1,0:T(8,128)S(1)}, f32[112,128]{1,0:T(8,128)S(1)}, u32[]{:S(2)}, u32[]{:S(2)}) collective-permute-start(f32[112,128]{1,0:T(8,128)S(1)} %get-tuple-element.17), channel_id=1, source_target_pairs={{0,56},{8,0},{16,8},{24,16},{32,24},{40,32},{48,40},{56,48},{1,57}... | collective-permute-start | bytes 172040 | tf_op jit(solution)/shard_map/ppermute | solution.py:402
  32.7 1.9 %collective-permute-start.6 = (f32[80,128]{1,0:T(8,128)S(1)}, f32[80,128]{1,0:T(8,128)S(1)}, u32[]{:S(2)}, u32[]{:S(2)}) collective-permute-start(f32[80,128]{1,0:T(8,128)S(1)} %shard_map.141.own_y_ref), channel_id=1, source_target_pairs={{0,7},{1,0},{2,1},{3,2},{4,3},{5,4},{6,5},{7,6},{8,15},{9,8},{10,9... | collective-permute-start | bytes 122888 | tf_op jit(solution)/shard_map/ppermute | solution.py:402
  32.9 4.6 %collective-permute-start.5 = (f32[80,128]{1,0:T(8,128)S(1)}, f32[80,128]{1,0:T(8,128)S(1)}, u32[]{:S(2)}, u32[]{:S(2)}) collective-permute-start(f32[80,128]{1,0:T(8,128)S(1)} %shard_map.141.own_y_ref), channel_id=1, source_target_pairs={{0,1},{1,2},{2,3},{3,4},{4,5},{5,6},{6,7},{7,0},{8,9},{9,10},{10,1... | collective-permute-start | bytes 122888 | tf_op jit(solution)/shard_map/ppermute | solution.py:402

commit v2 on v1

--- a/solution.py
+++ b/solution.py
@@ -9,13 +9,14 @@
 KEPT = 6
 WINDOW = CZ + 4
 ROWS = CZ * CX
-X_ROWS = 18
+FAR = 80
 MARKER = 3.0e38
 LIMIT = 1.0e30
 F32 = jnp.float32
 
 VMEM = pl.BlockSpec(memory_space=pltpu.VMEM)
 SMEM = pl.BlockSpec(memory_space=pltpu.SMEM)
+ANY = pl.BlockSpec(memory_space=pl.ANY)
 
 
 def lanes_of(rows):
@@ -34,84 +35,133 @@
     return row
 
 
-def kept(phases_ref, solutes_ref, c, z):
-    return phases_ref[c, z] if c < 3 else solutes_ref[c - 3, z]
-
-
-def pack_z(phases_ref, solutes_ref, flags_ref, down_ref, down2_ref, up_ref):
-    flags = [flag_row(flags_ref, b) for b in range(2)]
+LAYERS = (0, 1, 14, 15)
+STRIP = 24
+
+
+def gather(rows, value_of):
+    lane = lanes_of(rows)
+    packed = jnp.zeros((rows, 128), F32)
     for c in range(KEPT):
-        for z in range(CZ):
-            plane = kept(phases_ref, solutes_ref, c, z)
-            down_ref[c * CZ + z] = plane
-            if z < 2:
-                down2_ref[c * 2 + z] = plane
-            if z == CZ - 1:
-                up_ref[c] = plane
-    for b in range(2):
-        down_ref[KEPT * CZ, b * 8 : b * 8 + 8] = flags[b]
-        up_ref[KEPT, b * 8 : b * 8 + 8] = flags[b]
-
-
-def frame(
-    phases_ref, solutes_ref, above_ref, above2_ref, below_ref, flags_ref, melt_ref, shift_ref, slab_ref,
-    window_ref, low_ref, high_ref, raw_ref,
+        moved = pltpu.roll(value_of(c), 2 + 4 * c, 1)
+        packed = jnp.where((lane >= 4 * c) & (lane < 4 * c + 4), moved, packed)
+    return packed
+
+
+def pack_z(
+    phases_ref, solutes_ref, flags_ref, shift_ref, melt_ref,
+    bulk_ref, second_ref, last_ref, strip_ref, columns_ref, meta_ref,
+    flags_now, shift_now, melt_now, copied, small_copied,
 ):
-    slab = slab_ref[0]
-    shift = shift_ref[0]
-    at_bottom = slab == 0
-    at_top = slab == 3
+    copies = [
+        pltpu.make_async_copy(flags_ref, flags_now, small_copied.at[0]),
+        pltpu.make_async_copy(shift_ref, shift_now, small_copied.at[1]),
+        pltpu.make_async_copy(melt_ref, melt_now, small_copied.at[2]),
+    ]
     for c in range(KEPT):
-        fresh = jnp.full((CX, 128), 0.0 if c < 3 else melt_ref[c - 3], F32)
-        raw_ref[c, 0:CX] = below_ref[c]
-        for z in range(CZ):
-            raw_ref[c, (1 + z) * CX : (2 + z) * CX] = kept(phases_ref, solutes_ref, c, z)
-            raw_ref[c, (9 + z) * CX : (10 + z) * CX] = jnp.where(at_top, fresh, above_ref[c * CZ + z])
-        for z in range(2):
-            raw_ref[c, (17 + z) * CX : (18 + z) * CX] = jnp.where(slab >= 2, fresh, above2_ref[c * 2 + z])
-        for w in range(WINDOW):
-            start = pl.multiple_of((shift - 1 + w) * CX, CX)
-            window_ref[c, w * CX : (w + 1) * CX] = raw_ref[c, pl.ds(start, CX)]
-
-        @pl.when(at_bottom)
-        def _(c=c):
-            window_ref[c, CX : 2 * CX] = window_ref[c, 2 * CX : 3 * CX]
-
-        @pl.when(at_top)
-        def _(c=c):
-            window_ref[c, 10 * CX : 11 * CX] = window_ref[c, 9 * CX : 10 * CX]
-
-        for ref, near, far in ((low_ref, 0, 1), (high_ref, 15, 14)):
-            ref[c * X_ROWS : c * X_ROWS + 8] = window_ref[c, pl.ds(CX + near, 8, stride=CX)]
-            ref[c * X_ROWS + 8 : c * X_ROWS + 10] = window_ref[c, pl.ds(9 * CX + near, 2, stride=CX)]
-            ref[c * X_ROWS + 10 : c * X_ROWS + 18] = window_ref[c, pl.ds(2 * CX + far, 8, stride=CX)]
-    low_ref[KEPT * X_ROWS : KEPT * X_ROWS + 4] = flag_row(flags_ref, 0)[:4]
-    high_ref[KEPT * X_ROWS : KEPT * X_ROWS + 4] = flag_row(flags_ref, 1)[:4]
-
-
-def pack_y(window_ref, before_ref, after_ref, flags_ref, out_ref, inner_ref, ends_ref, sides_ref):
-    def gather(rows, value_of):
-        lane = lanes_of(rows)
-        packed = jnp.zeros((rows, 128), F32)
-        for c in range(KEPT):
-            moved = pltpu.roll(value_of(c), 2 + 4 * c, 1)
-            packed = jnp.where((lane >= 4 * c) & (lane < 4 * c + 4), moved, packed)
-        return packed
-
-    flags = jnp.concatenate([flag_row(flags_ref, b) for b in range(2)], axis=0)
+        source = phases_ref.at[c] if c < 3 else solutes_ref.at[c - 3]
+        copies.append(pltpu.make_async_copy(source, bulk_ref.at[pl.ds(c * ROWS, ROWS)], copied.at[c]))
+    for copy in copies:
+        copy.start()
+    for copy in copies:
+        copy.wait()
+
+    flags = jnp.concatenate([flag_row(flags_now, b) for b in range(2)], axis=0)
+    bulk_ref[KEPT * ROWS : KEPT * ROWS + CX] = flags
+    last_ref[KEPT * CX : (KEPT + 1) * CX] = flags
+    meta_ref[...] = jnp.zeros((8, 128), F32)
+    meta_ref[0:1] = jnp.full((1, 128), shift_now[0].astype(F32), F32)
+    for k in range(3):
+        meta_ref[1 + k : 2 + k] = jnp.full((1, 128), melt_now[k], F32)
+    for c in range(KEPT):
+        second_ref[2 * c * CX : 2 * (c + 1) * CX] = bulk_ref[c * ROWS : c * ROWS + 2 * CX]
+        last_ref[c * CX : (c + 1) * CX] = bulk_ref[c * ROWS + 7 * CX : (c + 1) * ROWS]
+        for n, x in enumerate(LAYERS):
+            strip_ref[pl.ds(n * KEPT + c, 8, stride=STRIP)] = bulk_ref[pl.ds(c * ROWS + x, 8, stride=CX)]
     flags = pltpu.roll(flags, 25, 1)
     flag_lane = (lanes_of(CX) == 24) | (lanes_of(CX) == 25)
     for z in range(CZ):
-        packed = gather(CX, lambda c: window_ref[c, (z + 2) * CX : (z + 3) * CX])
-        inner_ref[z * CX : (z + 1) * CX] = jnp.where(flag_lane, flags, packed)
-    ends_ref[...] = jnp.zeros((128, 128), F32)
-    ends_ref[0:CX] = gather(CX, lambda c: window_ref[c, CX : 2 * CX])
-    ends_ref[112:128] = gather(CX, lambda c: window_ref[c, 10 * CX : 11 * CX])
+        packed = gather(CX, lambda c: bulk_ref[c * ROWS + z * CX : c * ROWS + (z + 1) * CX])
+        columns_ref[z * CX : (z + 1) * CX] = jnp.where(flag_lane, flags, packed)
+    strip_ref[8 * STRIP : 8 * STRIP + 32] = columns_ref[...].T[0:32]
+
+
+def window_ends(meta_ref, slab_ref):
+    shift = jnp.max(meta_ref[0:1]).astype(jnp.int32)
+    slab = slab_ref[0]
+    return shift, jnp.where(slab == 0, shift, shift - 1), jnp.where(slab == 3, shift + 7, shift + 8)
+
+
+def pack_x(own_ref, above_ref, above2_ref, bulk_ref, meta_ref, slab_ref, low_ref, high_ref, raw_ref):
+    slab = slab_ref[0]
+    shift, first, last = window_ends(meta_ref, slab_ref)
+    fresh = jnp.zeros((STRIP, 128), F32)
+    sub = sublanes_of(STRIP) % KEPT
+    for k in range(3):
+        fresh = jnp.where(sub == 3 + k, meta_ref[1 + k : 2 + k], fresh)
+    raw_ref[0 : 8 * STRIP] = own_ref[0 : 8 * STRIP]
+    for z in range(CZ):
+        rows = slice((8 + z) * STRIP, (9 + z) * STRIP)
+        raw_ref[rows] = jnp.where(slab == 3, fresh, above_ref[z * STRIP : (z + 1) * STRIP])
+    for c in range(KEPT):
+        for n, x in enumerate(LAYERS):
+            at = 16 * STRIP + n * KEPT + c
+            raw_ref[at : at + 1] = above2_ref[2 * c * CX + x : 2 * c * CX + x + 1]
+
+    @pl.when(slab >= 2)
+    def _():
+        raw_ref[16 * STRIP : 17 * STRIP] = fresh
+
+    for i in range(10):
+        row = first if i == 0 else last if i == 9 else shift + (i - 1)
+        value = raw_ref[pl.ds(pl.multiple_of(row * STRIP, 8), STRIP)]
+        low_ref[i * 8 : i * 8 + KEPT] = value[0:6]
+        high_ref[i * 8 : i * 8 + KEPT] = value[18:24]
+        if 0 < i < 9:
+            low_ref[FAR + (i - 1) * 8 : FAR + (i - 1) * 8 + KEPT] = value[6:12]
+            high_ref[FAR + (i - 1) * 8 : FAR + (i - 1) * 8 + KEPT] = value[12:18]
+    low_ref[KEPT : KEPT + 1] = bulk_ref[KEPT * ROWS : KEPT * ROWS + 1]
+    high_ref[KEPT : KEPT + 1] = bulk_ref[KEPT * ROWS + 15 : KEPT * ROWS + 16]
+
+
+def turn_columns(columns_ref, above_ref, above2_ref, meta_ref, slab_ref, out_ref, raw_ref, wide_ref):
+    slab = slab_ref[0]
+    shift, first, last = window_ends(meta_ref, slab_ref)
+    fresh = jnp.zeros((CX, 128), F32)
+    part = lanes_of(CX) // 4
+    for k in range(3):
+        fresh = jnp.where(part == 3 + k, meta_ref[1 + k : 2 + k], fresh)
+    raw_ref[0:ROWS] = columns_ref[...]
+    wide_ref[...] = jnp.zeros((128, 128), F32)
+    wide_ref[0:32] = above_ref[8 * STRIP : 8 * STRIP + 32]
+    raw_ref[ROWS : 2 * ROWS] = wide_ref[...].T
+
+    @pl.when(slab == 3)
+    def _():
+        for z in range(CZ):
+            raw_ref[ROWS + z * CX : ROWS + (z + 1) * CX] = fresh
+
+    beyond = gather(CX, lambda c: above2_ref[2 * c * CX : (2 * c + 1) * CX])
+    raw_ref[2 * ROWS : 2 * ROWS + CX] = jnp.where(slab >= 2, fresh, beyond)
+
+    def rows_at(row):
+        return raw_ref[pl.ds(pl.multiple_of(row * CX, CX), CX)]
+
+    flag_lane = (lanes_of(CX) == 24) | (lanes_of(CX) == 25)
+    for z in range(CZ):
+        wide_ref[z * CX : (z + 1) * CX] = jnp.where(flag_lane, columns_ref[0:CX], rows_at(shift + z))
+    out_ref[0:32] = wide_ref[...].T[0:32]
+    wide_ref[...] = jnp.zeros((128, 128), F32)
+    wide_ref[0:CX] = rows_at(first)
+    wide_ref[112:128] = rows_at(last)
+    out_ref[32:56] = wide_ref[...].T[0:24]
+
+
+def pack_y(turned_ref, before_ref, after_ref, out_ref, sides_ref):
+    out_ref[0:56] = turned_ref[...]
     sides_ref[...] = jnp.zeros((128, 128), F32)
-    sides_ref[pl.ds(0, 8, stride=CX)] = gather(8, lambda c: before_ref[c * X_ROWS + 1 : c * X_ROWS + 9])
-    sides_ref[pl.ds(15, 8, stride=CX)] = gather(8, lambda c: after_ref[c * X_ROWS + 1 : c * X_ROWS + 9])
-    out_ref[0:32] = inner_ref[...].T[0:32]
-    out_ref[32:56] = ends_ref[...].T[0:24]
+    sides_ref[pl.ds(0, 8, stride=CX)] = gather(8, lambda c: before_ref[pl.ds(8 + c, 8, stride=8)])
+    sides_ref[pl.ds(15, 8, stride=CX)] = gather(8, lambda c: after_ref[pl.ds(8 + c, 8, stride=8)])
     out_ref[56:80] = sides_ref[...].T[0:24]
 
 
@@ -169,11 +219,11 @@
 
 
 def steps(
-    window_ref, before_ref, after_ref, own_y_ref, left_ref, right_ref, above_ref, below_ref,
-    flags_ref, slots_ref, slab_ref,
+    own_ref, above_ref, above2_ref, below_ref, before_ref, after_ref, own_y_ref, left_ref, right_ref, meta_ref,
+    slots_ref, slab_ref,
     stiffness_ref, barrier_ref, coupling_ref, slope_ref, diffusivity_ref, release_ref,
     phases_ref, solutes_ref, send_ref,
-    edge_ref, turned_ref, first_ref, xface_ref, final_ref,
+    raw_ref, window_ref, edge_ref, turned_ref, first_ref, xface_ref, final_ref,
 ):
     slab = slab_ref[0]
     at_bottom = slab == 0
@@ -185,7 +235,26 @@
         return (first_row + z + 0.5) / 32.0 - 0.5
 
     lane16, lane8, sub16 = lanes_of(CX), lanes_of(8), sublanes_of(CX)
-    flags = jnp.concatenate([flag_row(flags_ref, b) for b in range(2)], axis=0)
+    flags = own_ref[KEPT * ROWS : KEPT * ROWS + CX]
+
+    shift = jnp.max(meta_ref[0:1]).astype(jnp.int32)
+    for c in range(KEPT):
+        fresh = jnp.zeros((CX, 128), F32) + (meta_ref[c - 2 : c - 1] if c >= 3 else 0.0)
+        raw_ref[c, 0:CX] = below_ref[c * CX : (c + 1) * CX]
+        raw_ref[c, CX : 9 * CX] = own_ref[c * ROWS : (c + 1) * ROWS]
+        for z in range(CZ):
+            here = above_ref[c * ROWS + z * CX : c * ROWS + (z + 1) * CX]
+            raw_ref[c, (9 + z) * CX : (10 + z) * CX] = jnp.where(at_top, fresh, here)
+        for z in range(2):
+            here = above2_ref[(2 * c + z) * CX : (2 * c + z + 1) * CX]
+            raw_ref[c, (17 + z) * CX : (18 + z) * CX] = jnp.where(slab >= 2, fresh, here)
+        for w in range(WINDOW):
+            row = shift - 1 + w
+            if w == 1:
+                row = jnp.where(at_bottom, row + 1, row)
+            if w == WINDOW - 2:
+                row = jnp.where(at_top, row - 1, row)
+            window_ref[c, w * CX : (w + 1) * CX] = raw_ref[c, pl.ds(pl.multiple_of(row * CX, CX), CX)]
 
     edge_ref[...] = jnp.zeros((128, 128), F32)
     for group, start in ((0, 0), (1, 32), (2, 56)):
@@ -222,16 +291,16 @@
             [
                 beside_x(
                     window_ref, c, start,
-                    before_ref[c * X_ROWS + z + 1 : c * X_ROWS + z + 2],
-                    after_ref[c * X_ROWS + z + 1 : c * X_ROWS + z + 2],
+                    before_ref[(z + 1) * 8 + c : (z + 1) * 8 + c + 1],
+                    after_ref[(z + 1) * 8 + c : (z + 1) * 8 + c + 1],
                 )
                 for c in range(KEPT)
             ]
         )
         if z == -1:
-            rows, group, flag = turned_ref[0:CX], 1, below_ref[KEPT]
+            rows, group, flag = turned_ref[0:CX], 1, below_ref[KEPT * CX : (KEPT + 1) * CX]
         elif z == CZ:
-            rows, group, flag = turned_ref[112:128], 1, above_ref[KEPT * CZ]
+            rows, group, flag = turned_ref[112:128], 1, above_ref[KEPT * ROWS : KEPT * ROWS + CX]
         else:
             rows, group, flag = turned_ref[z * CX : (z + 1) * CX], 0, flags
         along_y = split([beside_y(own[c], rows, group * 12 + 2 * c) for c in range(KEPT)])
@@ -251,18 +320,18 @@
 
     face_height = height_of(sublanes_of(8).astype(F32))
     for side, ref, x in ((0, before_ref, 0), (1, after_ref, 15)):
-        own = [ref[c * X_ROWS + 1 : c * X_ROWS + 9] for c in range(KEPT)]
+        own = [ref[pl.ds(8 + c, 8, stride=8)] for c in range(KEPT)]
         along_z = (
-            [ref[c * X_ROWS + 2 : c * X_ROWS + 10] for c in range(KEPT)],
-            [ref[c * X_ROWS : c * X_ROWS + 8] for c in range(KEPT)],
+            [ref[pl.ds(16 + c, 8, stride=8)] for c in range(KEPT)],
+            [ref[pl.ds(c, 8, stride=8)] for c in range(KEPT)],
         )
         along_x = (
-            [ref[c * X_ROWS + 10 : c * X_ROWS + 18] for c in range(KEPT)],
+            [ref[pl.ds(FAR + c, 8, stride=8)] for c in range(KEPT)],
             [window_ref[c, pl.ds(2 * CX + x, 8, stride=CX)] for c in range(KEPT)],
         )
         rows = turned_ref[pl.ds(x, 8, stride=CX)]
         along_y = split([beside_y(own[c], rows, 24 + 2 * c) for c in range(KEPT)])
-        flag = ref[KEPT * X_ROWS : KEPT * X_ROWS + 1]
+        flag = ref[KEPT : KEPT + 1]
         result, _ = advance(own, (along_z, along_x, along_y), flag, face_height, par)
         for c in range(KEPT):
             xface_ref[side * KEPT + c] = result[c]
@@ -316,14 +385,14 @@
         along_y = split([beside_y(own[c], rows, 2 * c) for c in range(KEPT)])
         result, last = advance(own, (along_z, along_x, along_y), flags, height_of(z), par)
         for c in range(3):
-            phases_ref[c, z] = result[c]
-            solutes_ref[c, z] = result[3 + c]
-        phases_ref[3, z] = last
+            phases_ref[c, z * CX : (z + 1) * CX] = result[c]
+            solutes_ref[c, z * CX : (z + 1) * CX] = result[3 + c]
+        phases_ref[3, z * CX : (z + 1) * CX] = last
         for c in range(KEPT):
             final_ref[c * ROWS + z * CX : c * ROWS + (z + 1) * CX] = result[c]
 
     for owner in range(64):
-        send_ref[2 * owner, 0:1] = jnp.full((1, 128), MARKER, F32)
+        send_ref[owner, 0:1] = jnp.full((1, 128), MARKER, F32)
     group = lane8 // 8
     for b in range(2):
         for q in range(4):
@@ -341,38 +410,36 @@
                         swapped[i + step] = jnp.where(keep, pltpu.roll(one, 128 - step * 8, 1), two)
                 parts = swapped
             for d in range(16):
-                send_ref[slots_ref[b * 16 + d], 6 * q : 6 * q + 6] = parts[d][0:6]
-
-
-def place(arrived_ref, moved_ref):
+                slot = slots_ref[b * 16 + d]
+                send_ref[slot >> 1, pl.ds(2 * q + (slot & 1), KEPT, stride=8)] = parts[d][0:6]
+
+
+def place(arrived_ref, moved_ref, sources):
     sub16 = sublanes_of(16)
     weight = jnp.zeros((16, 128), F32)
     for i in range(16):
         weight = jnp.where((sub16 == i) & (lanes_of(16) == 0), float(2**i), weight)
     masks = []
     for block in range(4):
-        first = jnp.concatenate([arrived_ref[2 * (block * 16 + i), 0:1] for i in range(16)], axis=0)
+        first = jnp.concatenate([arrived_ref[block * 16 + i, 0:1] for i in range(16)], axis=0)
         masks.append(jnp.sum(jnp.where(first < LIMIT, weight, 0.0)).astype(jnp.int32))
     count = jnp.int32(0)
-    for block in range(4):
-
-        def one_source(i, count, block=block):
-            present = (masks[block] >> i) & 1
-            source = block * 16 + i
-
-            @pl.when((present == 1) & (count < 31))
-            def _():
-                for e in range(2):
-                    for q in range(4):
-                        part = arrived_ref[2 * source + e, 6 * q : 6 * q + 6]
-                        span = slice(q * 128, (q + 1) * 128)
-                        moved_ref[count + e, 0:3, span] = part[0:3]
-                        moved_ref[count + e, 3:4, span] = 1.0 - (part[0:1] + part[1:2] + part[2:3])
-                        moved_ref[count + e, 4:7, span] = part[3:6]
-
-            return count + 2 * present
-
-        count = lax.fori_loop(0, 16, one_source, count)
+    for source in range(64):
+        sources[count] = source
+        count = count + ((masks[source // 16] >> (source % 16)) & 1)
+    for n in range(0, 16, 4):
+        group = [sources[n + i] & 63 for i in range(4)]
+        rows = slice(2 * n, 2 * n + 8)
+        for q in range(4):
+            span = slice(q * 128, (q + 1) * 128)
+            parts = []
+            for c in range(KEPT):
+                at = 8 * c + 2 * q
+                parts.append(jnp.concatenate([arrived_ref[s, at : at + 2] for s in group], axis=0))
+            for c in range(3):
+                moved_ref[c, rows, span] = parts[c]
+                moved_ref[4 + c, rows, span] = parts[3 + c]
+            moved_ref[3, rows, span] = 1.0 - (parts[0] + parts[1] + parts[2])
 
 
 def shape_of(*dims):
@@ -415,38 +482,52 @@
     )
     slots = owner_list * 2 + earlier
 
-    down, down2, up = call(
+    bulk, second, last, strip, columns, meta = call(
         pack_z,
-        [VMEM, VMEM, SMEM],
-        [shape_of(KEPT * CZ + 1, CX, 128), shape_of(KEPT * 2, CX, 128), shape_of(KEPT + 1, CX, 128)],
-    )(phases, solutes, flags)
-    above = shifted(down, "gz", -1, False)
-    above2 = shifted(down2, "gz", -2, False)
-    below = shifted(up, "gz", 1, False)
-
-    window, low, high = call(
-        frame,
-        [VMEM] * 5 + [SMEM] * 4,
-        [shape_of(KEPT, WINDOW * CX, 128), shape_of(112, 128), shape_of(112, 128)],
-        [pltpu.VMEM((KEPT, 19 * CX, 128), F32)],
-    )(phases, solutes, above, above2, below, flags, melt, shift_rows, slab)
+        [ANY] * 5,
+        [
+            shape_of(KEPT * ROWS + CX, 128), shape_of(KEPT * 2 * CX, 128), shape_of((KEPT + 1) * CX, 128),
+            shape_of(8 * STRIP + 32, 128), shape_of(ROWS, 128), shape_of(8, 128),
+        ],
+        [
+            pltpu.SMEM((1, 1, 1, 32), jnp.int32), pltpu.SMEM((1,), jnp.int32), pltpu.SMEM((3,), F32),
+            pltpu.SemaphoreType.DMA((KEPT,)), pltpu.SemaphoreType.DMA((3,)),
+        ],
+    )(phases.reshape(4, ROWS, CY), solutes.reshape(3, ROWS, CY), flags, shift_rows, melt)
+    above_strip = shifted(strip, "gz", -1, False)
+    above2 = shifted(second, "gz", -2, False)
+    below = shifted(last, "gz", 1, False)
+    late_bulk, _ = lax.optimization_barrier((bulk, above_strip))
+    above = shifted(late_bulk, "gz", -1, False)
+
+    low, high = call(
+        pack_x,
+        [VMEM] * 5 + [SMEM],
+        [shape_of(FAR + 64, 128)] * 2,
+        [pltpu.VMEM((17 * STRIP, 128), F32)],
+    )(strip, above_strip, above2, bulk, meta, slab)
     before = shifted(high, "gx", 1, True)
     after = shifted(low, "gx", -1, True)
 
-    (faces,) = call(
-        pack_y,
-        [VMEM] * 3 + [SMEM],
-        [shape_of(80, 128)],
-        [pltpu.VMEM((128, 128), F32)] * 3,
-    )(window, before, after, flags)
+    (turned,) = call(
+        turn_columns,
+        [VMEM] * 4 + [SMEM],
+        [shape_of(56, 128)],
+        [pltpu.VMEM((17 * CX, 128), F32), pltpu.VMEM((128, 128), F32)],
+    )(columns, above_strip, above2, meta, slab)
+    (faces,) = call(pack_y, [VMEM] * 3, [shape_of(80, 128)], [pltpu.VMEM((128, 128), F32)])(
+        turned, before, after
+    )
     left = shifted(faces, "gy", 1, True)
     right = shifted(faces, "gy", -1, True)
 
     phases_out, solutes_out, send = call(
         steps,
-        [VMEM] * 8 + [SMEM] * 9,
-        [shape_of(4, CZ, CX, CY), shape_of(3, CZ, CX, CY), shape_of(128, 24, 128)],
+        [VMEM] * 10 + [SMEM] * 8,
+        [shape_of(4, ROWS, CY), shape_of(3, ROWS, CY), shape_of(64, 48, 128)],
         [
+            pltpu.VMEM((KEPT, 19 * CX, 128), F32),
+            pltpu.VMEM((KEPT, WINDOW * CX, 128), F32),
             pltpu.VMEM((128, 128), F32),
             pltpu.VMEM((128, 128), F32),
             pltpu.VMEM((KEPT, 10 * CX, 128), F32),
@@ -454,12 +535,16 @@
             pltpu.VMEM((8 * ROWS, 128), F32),
         ],
     )(
-        window, before, after, faces, left, right, above, below, flags, slots, slab,
+        bulk, above, above2, below, before, after, faces, left, right, meta, slots, slab,
         stiffness, barrier, coupling, slope, diffusivity, release,
     )
     arrived = lax.all_to_all(send, ("gx", "gy"), split_axis=0, concat_axis=0, tiled=True)
-    (moved,) = call(place, [VMEM], [shape_of(32, 7, 512)])(arrived)
-    return phases_out, solutes_out, moved
+    (moved,) = call(place, [VMEM], [shape_of(7, 32, 512)], [pltpu.SMEM((65,), jnp.int32)])(arrived)
+    return (
+        phases_out.reshape(4, CZ, CX, CY),
+        solutes_out.reshape(3, CZ, CX, CY),
+        jnp.transpose(moved, (1, 0, 2)),
+    )
 
 
 def solution(mesh):

time: 93.6 us -> 86.6 us (0.925)
  waiting for transfers between devices: 12.1 us -> 6.86 us
  local copies, waits for them, and re-layouts: 6.78 us -> 3.21 us
  starting transfers between devices: 15.3 us -> 17.5 us
    ppermute x7 -> x8, waiting for transfers between devices: 12.1 us -> 6.86 us  [shifted(): return lax.ppermute(value, axis, pairs)]
    unnamed x29 -> x22, local copies, waits for them, and re-layouts: 6.78 us -> 3.21 us
    ppermute x7 -> x8, starting transfers between devices: 15.3 us -> 17.5 us  [shifted(): return lax.ppermute(value, axis, pairs)]
    pallas_call x5 -> x6, Pallas kernels: 8.42 us -> 7.8 us  [the longest x1 5.23 us: per_device(): call(steps, [VMEM] * 10 + [SMEM] * 8, [shape_of(4, ROWS, CY), shape_of(3,...]
  transfers between devices with their start and end apart: 7 -> 8, of which waited for: 5 -> 5; matrix products, arithmetic and copies ran while one was open for 1% -> 1% of each run, Pallas kernels for 0% -> 1%
where the time goes in v2:
time: 86.6 us; the launch traced here: 86.3 us
  blocking collectives  48.6 us (56%)
  starting transfers between devices  17.5 us (20%)
  Pallas kernels  7.8 us (9%)
  waiting for transfers between devices  6.86 us (8%)
  local copies, waits for them, and re-layouts  3.21 us (4%)
  between operations  1.47 us (2%)
  other arithmetic  0.91 us (1%)
    all_to_all x1, blocking collectives, per_device(): lax.all_to_all(send, ('gx', 'gy'), split_axis=0, concat_axis=0, tiled=True)  48.6 us
    ppermute x8, starting transfers between devices, shifted(): return lax.ppermute(value, axis, pairs)  17.5 us
    ppermute x8, waiting for transfers between devices, shifted(): return lax.ppermute(value, axis, pairs)  6.86 us
    pallas_call x1, Pallas kernels, per_device(): call(steps, [VMEM] * 10 + [SMEM] * 8, [shape_of(4, ROWS, CY), shape_of(3,...  5.23 us
    unnamed x22, local copies, waits for them, and re-layouts  3.21 us
  transfers between devices with their start and end apart: 8, of which 5 were waited for; matrix products, arithmetic and copies ran while one was open for 1% of the time, Pallas kernels for 1%

profile of v2, /device:TPU:8, one launch (start us, length us, event | category | flops | bytes accessed | tf_op | source)
XLA Modules:
  0.0 86.3 jit_solution(13634280034686701593)
XLA Ops:
  0.6 0.0 copy-start.10
  1.4 0.9 %copy-done = f32[4,8,16,128]{3,2,1,0:T(8,128)S(1)} copy-done((f32[4,8,16,128]{3,2,1,0:T(8,128)S(1)}, f32[4,8,16,128]{3,2,1,0:T(8,128)}, u32[]{:S(2)}) %copy-start) | copy-done | bytes 262168
  2.3 0.9 %copy-done.1 = f32[3,8,16,128]{3,2,1,0:T(8,128)S(1)} copy-done((f32[3,8,16,128]{3,2,1,0:T(8,128)S(1)}, f32[3,8,16,128]{3,2,1,0:T(8,128)}, u32[]{:S(2)}) %copy-start.1) | copy-done | bytes 196632
  3.2 0.7 copy-done.8
  3.9 0.7 copy-done.9
  4.6 0.9 %shard_map.139 = (f32[784,128]{1,0:T(8,128)S(1)}, f32[192,128]{1,0:T(8,128)S(1)}, f32[112,128]{1,0:T(8,128)S(1)}, f32[224,128]{1,0:T(8,128)S(1)}, f32[128,128]{1,0:T(8,128)S(1)}, /*index=5*/f32[8,128]{1,0:T(8,128)S(1)}) custom-call(f32[4,128,128]{2,1,0:T(8,128)S(1)} %bitcast.8, f32[3,128,128]{2,1,0:T(8,128)S(1)} %bitcast.9, s32[1,1,1,32]{3,2,1,0:T(1,128)S(1)} %copy-done.8, ...), custom_call_target="tpu_custom_call" | custom-call | bytes 1000000 | tf_op jit(solution)/shard_map/pallas_call | solution.py:485
  5.5 4.1 %collective-permute-start = (f32[224,128]{1,0:T(8,128)S(1)}, f32[224,128]{1,0:T(8,128)S(1)}, u32[]{:S(2)}, u32[]{:S(2)}) collective-permute-start(f32[224,128]{1,0:T(8,128)S(1)} %get-tuple-element.16.own_ref), channel_id=1, source_target_pairs={{64,0},{128,64},{192,128},{65,1},{129,65},{193,129},{66,2},{130,66... | collective-permute-start | bytes 344072 | tf_op jit(solution)/shard_map/ppermute | solution.py:469
  9.6 1.3 %collective-permute-start.2 = (f32[192,128]{1,0:T(8,128)S(1)}, f32[192,128]{1,0:T(8,128)S(1)}, u32[]{:S(2)}, u32[]{:S(2)}) collective-permute-start(f32[192,128]{1,0:T(8,128)S(1)} %get-tuple-element.18), channel_id=1, source_target_pairs={{128,0},{192,64},{129,1},{193,65},{130,2},{194,66},{131,3},{195,67... | collective-permute-start | bytes 294920 | tf_op jit(solution)/shard_map/ppermute | solution.py:469
  10.9 1.4 %collective-permute-done.above_ref = f32[224,128]{1,0:T(8,128)S(1)} collective-permute-done((f32[224,128]{1,0:T(8,128)S(1)}, f32[224,128]{1,0:T(8,128)S(1)}, u32[]{:S(2)}, u32[]{:S(2)}) %collective-permute-start) | collective-permute-done | bytes 114720 | tf_op jit(solution)/shard_map/ppermute | solution.py:469
  12.3 4.0 %collective-permute-start.1 = (f32[784,128]{1,0:T(8,128)S(1)}, f32[784,128]{1,0:T(8,128)S(1)}, u32[]{:S(2)}, u32[]{:S(2)}) collective-permute-start(f32[784,128]{1,0:T(8,128)S(1)} %get-tuple-element.17.bulk_ref.own_ref), channel_id=1, source_target_pairs={{64,0},{128,64},{192,128},{65,1},{129,65},{193,129},{66,2},{130,66... | collective-permute-start | bytes 1204232 | tf_op jit(solution)/shard_map/ppermute | solution.py:469
  16.3 1.9 %collective-permute-start.3 = (f32[112,128]{1,0:T(8,128)S(1)}, f32[112,128]{1,0:T(8,128)S(1)}, u32[]{:S(2)}, u32[]{:S(2)}) collective-permute-start(f32[112,128]{1,0:T(8,128)S(1)} %get-tuple-element.19), channel_id=1, source_target_pairs={{0,64},{64,128},{128,192},{1,65},{65,129},{129,193},{2,66},{66,130... | collective-permute-start | bytes 172040 | tf_op jit(solution)/shard_map/ppermute | solution.py:469
  18.2 0.3 collective-permute-done.2.above2_ref
  18.5 0.1 shard_map.140
  18.6 1.6 %collective-permute-start.4 = (f32[144,128]{1,0:T(8,128)S(1)}, f32[144,128]{1,0:T(8,128)S(1)}, u32[]{:S(2)}, u32[]{:S(2)}) collective-permute-start(f32[144,128]{1,0:T(8,128)S(1)} %get-tuple-element.21), channel_id=1, source_target_pairs={{0,8},{8,16},{16,24},{24,32},{32,40},{40,48},{48,56},{56,0},{1,9},... | collective-permute-start | bytes 221192 | tf_op jit(solution)/shard_map/ppermute | solution.py:469
  20.3 4.0 %collective-permute-start.5 = (f32[144,128]{1,0:T(8,128)S(1)}, f32[144,128]{1,0:T(8,128)S(1)}, u32[]{:S(2)}, u32[]{:S(2)}) collective-permute-start(f32[144,128]{1,0:T(8,128)S(1)} %get-tuple-element.22), channel_id=1, source_target_pairs={{0,56},{8,0},{16,8},{24,16},{32,24},{40,32},{48,40},{56,48},{1,57}... | collective-permute-start | bytes 221192 | tf_op jit(solution)/shard_map/ppermute | solution.py:469
  24.3 0.9 %convert_reduce_fusion = s32[32]{0:T(128)S(1)} fusion(s32[32]{0:T(128)} %bitcast.13), kind=kLoop, calls=%fused_computation | loop fusion | flops 5088 | bytes 256 | tf_op jit(solution)/shard_map/reduce_sum | solution.py:479
  25.2 0.3 shard_map.141.turned_ref
  25.5 1.1 %collective-permute-done.4.before_ref = f32[144,128]{1,0:T(8,128)S(1)} collective-permute-done((f32[144,128]{1,0:T(8,128)S(1)}, f32[144,128]{1,0:T(8,128)S(1)}, u32[]{:S(2)}, u32[]{:S(2)}) %collective-permute-start.4) | collective-permute-done | bytes 73760 | tf_op jit(solution)/shard_map/ppermute | solution.py:469
  26.5 0.0 collective-permute-done.5.after_ref
  26.5 0.1 shard_map.142.own_y_ref
  26.7 0.0 collective-permute-start.7
  26.7 0.5 collective-permute-start.6
  27.2 0.0 collective-permute-done.3.below_ref
  27.2 1.2 %collective-permute-done.7.right_ref = f32[80,128]{1,0:T(8,128)S(1)} collective-permute-done((f32[80,128]{1,0:T(8,128)S(1)}, f32[80,128]{1,0:T(8,128)S(1)}, u32[]{:S(2)}, u32[]{:S(2)}) %collective-permute-start.7) | collective-permute-done | bytes 40992 | tf_op jit(solution)/shard_map/ppermute | solution.py:469
  28.4 3.0 %collective-permute-done.6.left_ref = f32[80,128]{1,0:T(8,128)S(1)} collective-permute-done((f32[80,128]{1,0:T(8,128)S(1)}, f32[80,128]{1,0:T(8,128)S(1)}, u32[]{:S(2)}, u32[]{:S(2)}) %collective-permute-start.6) | collective-permute-done | bytes 40992 | tf_op jit(solution)/shard_map/ppermute | solution.py:469
  31.3 0.0 collective-permute-done.1.above_ref
  31.4 0.0 copy-done.6
  31.4 0.0 copy-done.2
  31.4 0.0 copy-done.4
  31.4 5.2 %shard_map.143 = (f32[4,128,128]{2,1,0:T(8,128)}, f32[3,128,128]{2,1,0:T(8,128)}, f32[64,48,128]{2,1,0:T(8,128)S(1)}) custom-call(f32[784,128]{1,0:T(8,128)S(1)} %get-tuple-element.17.bulk_ref.own_ref, f32[784,128]{1,0:T(8,128)S(1)} %collective-permute-done.1.above_ref, f32[192,128]{1,0:T(8,128)S(1)} %collective-permute-done.2.above2_ref, ...), custom_call_target="tpu_custom_call" | custom-call | bytes 1000000 | tf_op jit(solution)/shard_map/pallas_call | solution.py:524
  36.6 48.6 %all_to_all.5.arrived_ref = f32[64,48,128]{2,1,0:T(8,128)S(1)} all-to-all(f32[64,48,128]{2,1,0:T(8,128)S(1)} %get-tuple-element.26), channel_id=1, replica_groups=mesh['gz'=4,'gx'=8,'gy'=8] {'gx','gy'}, dimensions={0} | all-to-all | bytes 3145728 | tf_op jit(solution)/shard_map/all_to_all | solution.py:541
  85.2 1.1 %shard_map.144 = f32[7,32,512]{2,1,0:T(8,128)} custom-call(f32[64,48,128]{2,1,0:T(8,128)S(1)} %all_to_all.5.arrived_ref), custom_call_target="tpu_custom_call" | custom-call | bytes 1000000 | tf_op jit(solution)/shard_map/pallas_call | solution.py:542
  (15 shorter events, 0.0 us)
Async XLA Ops:
  0.6 26.6 %copy-start.10 = (s32[1,1,1,32]{3,2,1,0:T(1,128)S(1)}, s32[1,1,1,32]{3,2,1,0:T(1,128)}, u32[]{:S(2)}) copy-start(s32[1,1,1,32]{3,2,1,0:T(1,128)} %param.17) | copy-start | bytes 388
  0.6 30.7 %copy-start.7 = (f32[4]{0:T(128)S(1)}, f32[4]{0:T(128)}, u32[]{:S(2)}) copy-start(f32[4]{0:T(128)} %slope_ref.1) | copy-start | bytes 52
  0.7 30.7 %copy-start.3 = (f32[4,3]{1,0:T(4,128)S(1)}, f32[4,3]{1,0:T(4,128)}, u32[]{:S(2)}) copy-start(f32[4,3]{1,0:T(4,128)} %coupling_ref.1) | copy-start | bytes 148
  0.7 30.7 %copy-start.6 = (f32[4]{0:T(128)S(1)}, f32[4]{0:T(128)}, u32[]{:S(2)}) copy-start(f32[4]{0:T(128)} %barrier_ref.1) | copy-start | bytes 52
  0.7 30.7 %copy-start.2 = (f32[4,3]{1,0:T(4,128)S(1)}, f32[4,3]{1,0:T(4,128)}, u32[]{:S(2)}) copy-start(f32[4,3]{1,0:T(4,128)} %stiffness_ref.1) | copy-start | bytes 148
  1.4 1.0 %copy-start = (f32[4,8,16,128]{3,2,1,0:T(8,128)S(1)}, f32[4,8,16,128]{3,2,1,0:T(8,128)}, u32[]{:S(2)}) copy-start(f32[4,8,16,128]{3,2,1,0:T(8,128)} %param.12) | copy-start | bytes 786436
  2.3 0.9 %copy-start.1 = (f32[3,8,16,128]{3,2,1,0:T(8,128)S(1)}, f32[3,8,16,128]{3,2,1,0:T(8,128)}, u32[]{:S(2)}) copy-start(f32[3,8,16,128]{3,2,1,0:T(8,128)} %param.13) | copy-start | bytes 589828
  3.2 0.7 copy-start.8
  3.9 0.7 copy-start.9
  4.6 26.8 %copy-start.4 = (f32[4,3]{1,0:T(4,128)S(1)}, f32[4,3]{1,0:T(4,128)}, u32[]{:S(2)}) copy-start(f32[4,3]{1,0:T(4,128)} %diffusivity_ref.1) | copy-start | bytes 148
  4.6 26.8 %copy-start.5 = (f32[4,3]{1,0:T(4,128)S(1)}, f32[4,3]{1,0:T(4,128)}, u32[]{:S(2)}) copy-start(f32[4,3]{1,0:T(4,128)} %release_ref.1) | copy-start | bytes 148
  5.5 6.8 %collective-permute-start = (f32[224,128]{1,0:T(8,128)S(1)}, f32[224,128]{1,0:T(8,128)S(1)}, u32[]{:S(2)}, u32[]{:S(2)}) collective-permute-start(f32[224,128]{1,0:T(8,128)S(1)} %get-tuple-element.16.own_ref), channel_id=1, source_target_pairs={{64,0},{128,64},{192,128},{65,1},{129,65},{193,129},{66,2},{130,66... | collective-permute-start | bytes 344072 | tf_op jit(solution)/shard_map/ppermute | solution.py:469
  9.6 8.9 %collective-permute-start.2 = (f32[192,128]{1,0:T(8,128)S(1)}, f32[192,128]{1,0:T(8,128)S(1)}, u32[]{:S(2)}, u32[]{:S(2)}) collective-permute-start(f32[192,128]{1,0:T(8,128)S(1)} %get-tuple-element.18), channel_id=1, source_target_pairs={{128,0},{192,64},{129,1},{193,65},{130,2},{194,66},{131,3},{195,67... | collective-permute-start | bytes 294920 | tf_op jit(solution)/shard_map/ppermute | solution.py:469
  12.3 19.1 %collective-permute-start.1 = (f32[784,128]{1,0:T(8,128)S(1)}, f32[784,128]{1,0:T(8,128)S(1)}, u32[]{:S(2)}, u32[]{:S(2)}) collective-permute-start(f32[784,128]{1,0:T(8,128)S(1)} %get-tuple-element.17.bulk_ref.own_ref), channel_id=1, source_target_pairs={{64,0},{128,64},{192,128},{65,1},{129,65},{193,129},{66,2},{130,66... | collective-permute-start | bytes 1204232 | tf_op jit(solution)/shard_map/ppermute | solution.py:469
  16.3 11.0 %collective-permute-start.3 = (f32[112,128]{1,0:T(8,128)S(1)}, f32[112,128]{1,0:T(8,128)S(1)}, u32[]{:S(2)}, u32[]{:S(2)}) collective-permute-start(f32[112,128]{1,0:T(8,128)S(1)} %get-tuple-element.19), channel_id=1, source_target_pairs={{0,64},{64,128},{128,192},{1,65},{65,129},{129,193},{2,66},{66,130... | collective-permute-start | bytes 172040 | tf_op jit(solution)/shard_map/ppermute | solution.py:469
  18.6 7.9 %collective-permute-start.4 = (f32[144,128]{1,0:T(8,128)S(1)}, f32[144,128]{1,0:T(8,128)S(1)}, u32[]{:S(2)}, u32[]{:S(2)}) collective-permute-start(f32[144,128]{1,0:T(8,128)S(1)} %get-tuple-element.21), channel_id=1, source_target_pairs={{0,8},{8,16},{16,24},{24,32},{32,40},{40,48},{48,56},{56,0},{1,9},... | collective-permute-start | bytes 221192 | tf_op jit(solution)/shard_map/ppermute | solution.py:469
  20.3 6.3 %collective-permute-start.5 = (f32[144,128]{1,0:T(8,128)S(1)}, f32[144,128]{1,0:T(8,128)S(1)}, u32[]{:S(2)}, u32[]{:S(2)}) collective-permute-start(f32[144,128]{1,0:T(8,128)S(1)} %get-tuple-element.22), channel_id=1, source_target_pairs={{0,56},{8,0},{16,8},{24,16},{32,24},{40,32},{48,40},{56,48},{1,57}... | collective-permute-start | bytes 221192 | tf_op jit(solution)/shard_map/ppermute | solution.py:469
  26.7 1.7 %collective-permute-start.7 = (f32[80,128]{1,0:T(8,128)S(1)}, f32[80,128]{1,0:T(8,128)S(1)}, u32[]{:S(2)}, u32[]{:S(2)}) collective-permute-start(f32[80,128]{1,0:T(8,128)S(1)} %shard_map.142.own_y_ref), channel_id=1, source_target_pairs={{0,7},{1,0},{2,1},{3,2},{4,3},{5,4},{6,5},{7,6},{8,15},{9,8},{10,9... | collective-permute-start | bytes 122888 | tf_op jit(solution)/shard_map/ppermute | solution.py:469
  26.7 4.7 %collective-permute-start.6 = (f32[80,128]{1,0:T(8,128)S(1)}, f32[80,128]{1,0:T(8,128)S(1)}, u32[]{:S(2)}, u32[]{:S(2)}) collective-permute-start(f32[80,128]{1,0:T(8,128)S(1)} %shard_map.142.own_y_ref), channel_id=1, source_target_pairs={{0,1},{1,2},{2,3},{3,4},{4,5},{5,6},{6,7},{7,0},{8,9},{9,10},{10,1... | collective-permute-start | bytes 122888 | tf_op jit(solution)/shard_map/ppermute | solution.py:469

commit v3 on v2

v3 whole, which is shorter than its diff:
```python
import jax
import jax.numpy as jnp
from jax import lax
from jax.experimental import pallas as pl
from jax.experimental.pallas import tpu as pltpu
from jax.sharding import PartitionSpec as P

CZ, CX, CY = 8, 16, 128
KEPT = 6
HELD = KEPT + 3
WINDOW = CZ + 4
ROWS = CZ * CX
X_ROWS = 18
MARKER = 3.0e38
LIMIT = 1.0e30
F32 = jnp.float32

VMEM = pl.BlockSpec(memory_space=pltpu.VMEM)
SMEM = pl.BlockSpec(memory_space=pltpu.SMEM)


def lanes_of(rows):
    return lax.broadcasted_iota(jnp.int32, (rows, 128), 1)


def sublanes_of(rows):
    return lax.broadcasted_iota(jnp.int32, (rows, 128), 0)


def flag_row(small_ref, b):
    group = lanes_of(8) // 8
    row = jnp.zeros((8, 128), F32)
    for d in range(16):
        row = jnp.where(group == d, small_ref[b * 16 + d].astype(F32), row)
    return row


LAYERS = (0, 1, 14, 15)
STRIP = 24
PAIRED = 8 * STRIP + 32


def gather(rows, value_of):
    lane = lanes_of(rows)
    packed = jnp.zeros((rows, 128), F32)
    for c in range(KEPT):
        moved = pltpu.roll(value_of(c), 2 + 4 * c, 1)
        packed = jnp.where((lane >= 4 * c) & (lane < 4 * c + 4), moved, packed)
    return packed


def pack_z(
    phases_ref, solutes_ref, small_ref, slab_ref,
    bulk_ref, second_ref, early_ref, even_ref, odd_ref, strip_ref, columns_ref, meta_ref,
    last_ref,
):
    flags = jnp.concatenate([flag_row(small_ref, b) for b in range(2)], axis=0)
    bulk_ref[KEPT * ROWS : KEPT * ROWS + CX] = flags
    last_ref[KEPT * CX : (KEPT + 1) * CX] = flags
    meta_ref[0:8] = jnp.full((8, 128), small_ref[32].astype(F32), F32)
    meta_ref[8:24] = flags
    for c in range(KEPT):
        source = phases_ref.at[c] if c < 3 else solutes_ref.at[c - 3]
        bulk_ref[c * ROWS : (c + 1) * ROWS] = source[...]
        second_ref[2 * c * CX : 2 * (c + 1) * CX] = bulk_ref[c * ROWS : c * ROWS + 2 * CX]
        last_ref[c * CX : (c + 1) * CX] = bulk_ref[c * ROWS + 7 * CX : (c + 1) * ROWS]
        for n, x in enumerate(LAYERS):
            strip_ref[pl.ds(n * KEPT + c, 8, stride=STRIP)] = bulk_ref[pl.ds(c * ROWS + x, 8, stride=CX)]
            early_ref[n * KEPT + c : n * KEPT + c + 1] = bulk_ref[c * ROWS + x : c * ROWS + x + 1]
    flags = pltpu.roll(flags, 25, 1)
    flag_lane = (lanes_of(CX) == 24) | (lanes_of(CX) == 25)
    for z in range(CZ):
        packed = gather(CX, lambda c: bulk_ref[c * ROWS + z * CX : c * ROWS + (z + 1) * CX])
        columns_ref[z * CX : (z + 1) * CX] = jnp.where(flag_lane, flags, packed)
    early_ref[STRIP : STRIP + CX] = columns_ref[0:CX]
    strip_ref[8 * STRIP : PAIRED] = columns_ref[...].T[0:32]
    is_even = (slab_ref[0] & 1) == 0
    last_ref[(KEPT + 1) * CX : PAIRED] = jnp.zeros((PAIRED - (KEPT + 1) * CX, 128), F32)
    even_ref[...] = jnp.where(is_even, last_ref[...], strip_ref[...])
    odd_ref[...] = jnp.where(is_even, strip_ref[...], last_ref[...])


def melt_of(row_ref, k):
    row = row_ref[...]
    lane = lax.broadcasted_iota(jnp.int32, row.shape, 1)
    return jnp.sum(jnp.where(lane == k, row, 0.0), axis=1, keepdims=True)


def window_ends(meta_ref, slab_ref):
    shift = jnp.max(meta_ref[0:1]).astype(jnp.int32)
    slab = slab_ref[0]
    return shift, jnp.where(slab == 0, shift, shift - 1), jnp.where(slab == 3, shift + 7, shift + 8)


def pack_x(own_ref, even_ref, odd_ref, above2_ref, meta_ref, row_ref, slab_ref, low_ref, high_ref, raw_ref):
    slab = slab_ref[0]
    shift, first, last = window_ends(meta_ref, slab_ref)
    fresh = jnp.zeros((STRIP, 128), F32)
    sub = sublanes_of(STRIP) % KEPT
    for k in range(3):
        fresh = jnp.where(sub == 3 + k, melt_of(row_ref, k), fresh)
    raw_ref[0 : 8 * STRIP] = own_ref[0 : 8 * STRIP]
    for z in range(CZ):
        rows = slice(z * STRIP, (z + 1) * STRIP)
        here = jnp.where((slab & 1) == 0, even_ref[rows], odd_ref[rows])
        raw_ref[(8 + z) * STRIP : (9 + z) * STRIP] = jnp.where(slab == 3, fresh, here)
    raw_ref[16 * STRIP : 17 * STRIP] = above2_ref[0:STRIP]

    @pl.when(slab >= 2)
    def _():
        raw_ref[16 * STRIP : 17 * STRIP] = fresh

    for i in range(10):
        row = first if i == 0 else last if i == 9 else shift + (i - 1)
        value = raw_ref[pl.ds(pl.multiple_of(row * STRIP, 8), STRIP)]
        low_ref[pl.ds(i, KEPT, stride=X_ROWS)] = value[0:6]
        high_ref[pl.ds(i, KEPT, stride=X_ROWS)] = value[18:24]
        if 0 < i < 9:
            low_ref[pl.ds(9 + i, KEPT, stride=X_ROWS)] = value[6:12]
            high_ref[pl.ds(9 + i, KEPT, stride=X_ROWS)] = value[12:18]
    flags = meta_ref[8:24]
    low_ref[KEPT * X_ROWS : KEPT * X_ROWS + 4] = flags[0:4]
    high_ref[KEPT * X_ROWS : KEPT * X_ROWS + 4] = flags[12:16]


def turn_columns(
    columns_ref, even_ref, odd_ref, above2_ref, meta_ref, row_ref, slab_ref, balance_ref,
    out_ref, slots_ref, raw_ref, wide_ref, given_ref,
):
    for owner in range(64):
        given_ref[owner] = jnp.int32(0)
    for t in range(32):
        owner = balance_ref[0, 0, 0, t]
        slots_ref[t] = 2 * owner + given_ref[owner]
        given_ref[owner] = jnp.int32(1)

    slab = slab_ref[0]
    shift, first, last = window_ends(meta_ref, slab_ref)
    fresh = jnp.zeros((CX, 128), F32)
    part = lanes_of(CX) // 4
    for k in range(3):
        fresh = jnp.where(part == 3 + k, melt_of(row_ref, k), fresh)
    raw_ref[0:ROWS] = columns_ref[...]
    wide_ref[...] = jnp.zeros((128, 128), F32)
    wide_ref[0:32] = jnp.where((slab & 1) == 0, even_ref[8 * STRIP : PAIRED], odd_ref[8 * STRIP : PAIRED])
    raw_ref[ROWS : 2 * ROWS] = wide_ref[...].T

    @pl.when(slab == 3)
    def _():
        for z in range(CZ):
            raw_ref[ROWS + z * CX : ROWS + (z + 1) * CX] = fresh

    raw_ref[2 * ROWS : 2 * ROWS + CX] = jnp.where(slab >= 2, fresh, above2_ref[STRIP : STRIP + CX])

    def rows_at(row):
        return raw_ref[pl.ds(pl.multiple_of(row * CX, CX), CX)]

    flag_lane = (lanes_of(CX) == 24) | (lanes_of(CX) == 25)
    for z in range(CZ):
        wide_ref[z * CX : (z + 1) * CX] = jnp.where(flag_lane, columns_ref[0:CX], rows_at(shift + z))
    out_ref[0:32] = wide_ref[...].T[0:32]
    wide_ref[...] = jnp.zeros((128, 128), F32)
    wide_ref[0:CX] = rows_at(first)
    wide_ref[112:128] = rows_at(last)
    out_ref[32:56] = wide_ref[...].T[0:24]


def pack_y(turned_ref, before_ref, after_ref, up_ref, down_ref, sides_ref):
    sides_ref[...] = jnp.zeros((128, 128), F32)
    sides_ref[pl.ds(0, 8, stride=CX)] = gather(8, lambda c: before_ref[c * X_ROWS + 1 : c * X_ROWS + 9])
    sides_ref[pl.ds(15, 8, stride=CX)] = gather(8, lambda c: after_ref[c * X_ROWS + 1 : c * X_ROWS + 9])
    sides_ref[...] = sides_ref[...].T
    for ref, near, far in ((up_ref, 1, 0), (down_ref, 2, 3)):
        ref[0:6] = turned_ref[pl.ds(near, KEPT, stride=4)]
        ref[6:12] = turned_ref[pl.ds(far, KEPT, stride=4)]
        ref[12:18] = turned_ref[pl.ds(32 + near, KEPT, stride=4)]
        ref[18:24] = sides_ref[pl.ds(near, KEPT, stride=4)]
        ref[24:25] = turned_ref[23 + near : 24 + near]


def read_parameters(table_ref, plain_ref):
    stiffness = [[table_ref[a, e] for e in range(3)] for a in range(4)]
    return dict(
        stiffness=stiffness,
        total=[row[0] + row[1] + row[2] for row in stiffness],
        coupling=[[table_ref[a, 3 + k] for k in range(3)] for a in range(4)],
        base=[0.5 * table_ref[3, 6 + k] for k in range(3)],
        excess=[[0.5 * (table_ref[a, 6 + k] - table_ref[3, 6 + k]) for k in range(3)] for a in range(3)],
        release=[[table_ref[a, 9 + k] for k in range(3)] for a in range(4)],
        barrier=[plain_ref[3 + a] for a in range(4)],
        twice=[2.0 * plain_ref[3 + a] for a in range(4)],
        slope=[plain_ref[7 + a] for a in range(4)],
    )


def with_densities(kept_values, par):
    p = kept_values[:3]
    return list(kept_values) + [
        par["base"][k] + (par["excess"][0][k] * p[0] + par["excess"][1][k] * p[1] + par["excess"][2][k] * p[2])
        for k in range(3)
    ]


def flows(own, beside):
    return [(own[6 + k] + beside[6 + k]) * (beside[3 + k] - own[3 + k]) for k in range(3)]


def advance(own, neighbours, flag, height, par, flow_below=None):
    others = own[0] + own[1] + own[2]
    fractions = [own[0], own[1], own[2], 1.0 - others]
    solutes = own[3:6]
    stiffness = par["stiffness"]
    total = par["total"]
    laplace = [(-2.0 * total[a]) * own[a] for a in range(3)] + [(2.0 * total[3]) * others]
    gains = None
    flow_above = None
    for e, (upper, lower) in enumerate(neighbours):
        sums = [upper[a] + lower[a] for a in range(3)]
        for a in range(3):
            laplace[a] = laplace[a] + stiffness[a][e] * sums[a]
        laplace[3] = laplace[3] - stiffness[3][e] * (sums[0] + sums[1] + sums[2])
        gained = flows(own, upper)
        if e == 0:
            flow_above = gained
        if e == 0 and flow_below is not None:
            gained = [gained[k] - flow_below[k] for k in range(3)]
        else:
            more = flows(own, lower)
            gained = [gained[k] + more[k] for k in range(3)]
        gains = gained if e == 0 else [gains[k] + gained[k] for k in range(3)]
    rates = []
    for a in range(4):
        p = fractions[a]
        drive = (par["slope"][a] * height - par["barrier"][a]) + par["twice"][a] * p
        for k in range(3):
            drive = drive + par["coupling"][a][k] * solutes[k]
        rates.append(flag * (laplace[a] + (p - p * p) * drive))
    mean = 0.25 * ((rates[0] + rates[1]) + (rates[2] + rates[3]))
    changes = [rate - mean for rate in rates]
    after = [fractions[a] + changes[a] for a in range(4)]
    for k in range(3):
        released = par["release"][0][k] * changes[0]
        for a in range(1, 4):
            released = released + par["release"][a][k] * changes[a]
        after.append(solutes[k] + (gains[k] + released))
    return after[:3] + after[4:], after[3], flow_above


def steps(
    own_ref, above_ref, above2_ref, even_ref, odd_ref, before_ref, after_ref, own_y_ref, left_ref, right_ref, meta_ref,
    slots_ref, slab_ref, plain_ref, table_ref,
    phases_ref, solutes_ref, send_ref,
    raw_ref, window_ref, edge_ref, turned_ref, first_ref, side_ref, xface_ref, final_ref,
):
    slab = slab_ref[0]
    at_bottom = slab == 0
    at_top = slab == 3
    par = read_parameters(table_ref, plain_ref)
    first_row = (slab * CZ).astype(F32)

    def height_of(z):
        return (first_row + z + 0.5) / 32.0 - 0.5

    lane16, lane8, sub16 = lanes_of(CX), lanes_of(8), sublanes_of(CX)
    flags = own_ref[KEPT * ROWS : KEPT * ROWS + CX]

    def below(c):
        rows = slice(c * CX, (c + 1) * CX)
        return jnp.where((slab & 1) == 0, odd_ref[rows], even_ref[rows])

    shift = jnp.max(meta_ref[0:1]).astype(jnp.int32)
    for c in range(KEPT):
        fresh = jnp.full((CX, 128), plain_ref[c - 3] if c >= 3 else 0.0, F32)
        raw_ref[c, 0:CX] = below(c)
        raw_ref[c, CX : 9 * CX] = own_ref[c * ROWS : (c + 1) * ROWS]
        for z in range(CZ):
            here = above_ref[c * ROWS + z * CX : c * ROWS + (z + 1) * CX]
            raw_ref[c, (9 + z) * CX : (10 + z) * CX] = jnp.where(at_top, fresh, here)
        for z in range(2):
            here = above2_ref[(2 * c + z) * CX : (2 * c + z + 1) * CX]
            raw_ref[c, (17 + z) * CX : (18 + z) * CX] = jnp.where(slab >= 2, fresh, here)
        for w in range(WINDOW):
            row = shift - 1 + w
            if w == 1:
                row = jnp.where(at_bottom, row + 1, row)
            if w == WINDOW - 2:
                row = jnp.where(at_top, row - 1, row)
            window_ref[c, w * CX : (w + 1) * CX] = raw_ref[c, pl.ds(pl.multiple_of(row * CX, CX), CX)]

    for w in range(WINDOW):
        rows = slice(w * CX, (w + 1) * CX)
        held = with_densities([window_ref[c, rows] for c in range(KEPT)], par)
        for c in range(KEPT, HELD):
            window_ref[c, rows] = held[c]
    for side, ref in ((0, before_ref), (1, after_ref)):
        held = with_densities([ref[c * X_ROWS : (c + 1) * X_ROWS] for c in range(KEPT)], par)
        for c in range(HELD):
            side_ref[side * HELD + c, 0:X_ROWS] = held[c]

    edge_ref[...] = jnp.zeros((128, 128), F32)
    for group, start in ((0, 0), (1, 12), (2, 18)):
        for ref, odd_row in ((right_ref, 0), (left_ref, 1)):
            held = with_densities([ref[start + c : start + c + 1] for c in range(KEPT)], par)
            for c in range(HELD):
                at = group * 2 * HELD + 2 * c + odd_row
                edge_ref[at : at + 1] = held[c]
    turned_ref[...] = edge_ref[...].T

    def beside_y(value, rows, column):
        lane = lane16 if value.shape[0] == CX else lane8
        fill = pltpu.roll(rows, 127 - column, 1)
        upper = jnp.where(lane == 127, fill, pltpu.roll(value, 127, 1))
        lower = jnp.where(lane == 0, fill, pltpu.roll(value, 1, 1))
        return upper, lower

    def beside_x(ref, c, start, low_row, high_row):
        upper = jnp.where(sub16 == 15, high_row, ref[c, start + 1 : start + 1 + CX])
        lower = jnp.where(sub16 == 0, low_row, ref[c, start - 1 : start - 1 + CX])
        return upper, lower

    def split(pairs):
        return ([pair[0] for pair in pairs], [pair[1] for pair in pairs])

    def store_held(ref, rows, values):
        for c, value in enumerate(with_densities(values, par)):
            ref[c, rows] = value

    flow = None
    for w in range(1, WINDOW - 1):
        z = w - 2
        start = w * CX
        own = [window_ref[c, start : start + CX] for c in range(HELD)]
        along_z = (
            [window_ref[c, start + CX : start + 2 * CX] for c in range(HELD)],
            [window_ref[c, start - CX : start] for c in range(HELD)],
        )
        along_x = split(
            [
                beside_x(
                    window_ref, c, start,
                    side_ref[c, z + 1 : z + 2], side_ref[HELD + c, z + 1 : z + 2],
                )
                for c in range(HELD)
            ]
        )
        if z == -1:
            rows, group, flag = turned_ref[0:CX], 1, below(KEPT)
        elif z == CZ:
            rows, group, flag = turned_ref[112:128], 1, above_ref[KEPT * ROWS : KEPT * ROWS + CX]
        else:
            rows, group, flag = turned_ref[z * CX : (z + 1) * CX], 0, flags
        along_y = split([beside_y(own[c], rows, 2 * (group * HELD + c)) for c in range(HELD)])
        result, _, flow = advance(own, (along_z, along_x, along_y), flag, height_of(z), par, flow)
        store_held(first_ref, slice((w - 1) * CX, w * CX), result)

    @pl.when(at_bottom)
    def _():
        for c in range(HELD):
            first_ref[c, 0:CX] = first_ref[c, CX : 2 * CX]

    @pl.when(at_top)
    def _():
        for c in range(HELD):
            first_ref[c, 9 * CX : 10 * CX] = first_ref[c, 8 * CX : 9 * CX]

    face_height = height_of(sublanes_of(8).astype(F32))
    for side, ref, x in ((0, before_ref, 0), (1, after_ref, 15)):
        layers = [side_ref.at[side * HELD + c] for c in range(HELD)]
        own = [layer[1:9] for layer in layers]
        along_z = ([layer[2:10] for layer in layers], [layer[0:8] for layer in layers])
        along_x = (
            [layer[10:18] for layer in layers],
            [window_ref[c, pl.ds(2 * CX + x, 8, stride=CX)] for c in range(HELD)],
        )
        rows = turned_ref[pl.ds(x, 8, stride=CX)]
        along_y = split([beside_y(own[c], rows, 2 * (2 * HELD + c)) for c in range(HELD)])
        at = KEPT * X_ROWS + (3 if side == 0 else 0)
        flag = ref[at : at + 1]
        result, _, _ = advance(own, (along_z, along_x, along_y), flag, face_height, par)
        for c, value in enumerate(with_densities(result, par)):
            xface_ref[side * HELD + c] = value

    sub8 = sublanes_of(8)

    def both(right_row, left_row):
        return jnp.where(sub8 == 0, right_row, left_row)

    def lifted(c, start):
        return both(right_ref[start + c : start + c + 1], left_ref[start + c : start + c + 1])

    own, ends, sides, outer = [
        with_densities([lifted(c, start) for c in range(KEPT)], par) for start in (0, 12, 18, 6)
    ]
    inner = with_densities(
        [both(own_y_ref[4 * c + 1 : 4 * c + 2], own_y_ref[4 * c + 2 : 4 * c + 3]) for c in range(KEPT)], par
    )
    along_z = (
        [jnp.where(lane8 >= 112, ends[c], pltpu.roll(own[c], 112, 1)) for c in range(HELD)],
        [jnp.where(lane8 < 16, ends[c], pltpu.roll(own[c], 16, 1)) for c in range(HELD)],
    )
    along_x = (
        [jnp.where(lane8 % 16 == 15, sides[c], pltpu.roll(own[c], 127, 1)) for c in range(HELD)],
        [jnp.where(lane8 % 16 == 0, sides[c], pltpu.roll(own[c], 1, 1)) for c in range(HELD)],
    )
    flag = both(right_ref[24:25], left_ref[24:25])
    result, _, _ = advance(
        own, (along_z, along_x, (outer, inner)), flag, height_of((lane8 // 16).astype(F32)), par
    )
    for c, value in enumerate(with_densities(result, par)):
        edge_ref[2 * c : 2 * c + 2] = value[0:2]
    turned_ref[...] = edge_ref[...].T

    flow = None
    for z in range(CZ):
        start = (z + 1) * CX
        own = [first_ref[c, start : start + CX] for c in range(HELD)]
        along_z = (
            [first_ref[c, start + CX : start + 2 * CX] for c in range(HELD)],
            [first_ref[c, start - CX : start] for c in range(HELD)],
        )
        along_x = split(
            [
                beside_x(first_ref, c, start, xface_ref[c, z : z + 1], xface_ref[HELD + c, z : z + 1])
                for c in range(HELD)
            ]
        )
        rows = turned_ref[z * CX : (z + 1) * CX]
        along_y = split([beside_y(own[c], rows, 2 * c) for c in range(HELD)])
        result, last, flow = advance(own, (along_z, along_x, along_y), flags, height_of(z), par, flow)
        for c in range(3):
            phases_ref[c, z * CX : (z + 1) * CX] = result[c]
            solutes_ref[c, z * CX : (z + 1) * CX] = result[3 + c]
        phases_ref[3, z * CX : (z + 1) * CX] = last
        for c in range(KEPT):
            final_ref[c * ROWS + z * CX : c * ROWS + (z + 1) * CX] = result[c]

    for owner in range(64):
        send_ref[owner, 0:1] = jnp.full((1, 128), MARKER, F32)
    group = lane8 // 8
    for b in range(2):
        for q in range(4):
            parts = []
            for i in range(16):
                row = (2 * q + i // 8) * CX + b * 8 + i % 8
                parts.append(final_ref[pl.ds(row, 8, stride=ROWS)])
            for step in (8, 4, 2, 1):
                keep = (group & step) == 0
                swapped = list(parts)
                for i in range(16):
                    if i & step == 0:
                        one, two = parts[i], parts[i + step]
                        swapped[i] = jnp.where(keep, one, pltpu.roll(two, step * 8, 1))
                        swapped[i + step] = jnp.where(keep, pltpu.roll(one, 128 - step * 8, 1), two)
                parts = swapped
            for d in range(16):
                slot = slots_ref[b * 16 + d]
                send_ref[slot >> 1, pl.ds(2 * q + (slot & 1), KEPT, stride=8)] = parts[d][0:6]


def place(arrived_ref, moved_ref, sources):
    sub16 = sublanes_of(16)
    weight = jnp.zeros((16, 128), F32)
    for i in range(16):
        weight = jnp.where((sub16 == i) & (lanes_of(16) == 0), float(2**i), weight)
    masks = []
    for block in range(4):
        first = jnp.concatenate([arrived_ref[block * 16 + i, 0:1] for i in range(16)], axis=0)
        masks.append(jnp.sum(jnp.where(first < LIMIT, weight, 0.0)).astype(jnp.int32))
    count = jnp.int32(0)
    for source in range(64):
        sources[count] = source
        count = count + ((masks[source // 16] >> (source % 16)) & 1)
    for n in range(0, 16, 4):
        group = [sources[n + i] & 63 for i in range(4)]
        rows = slice(2 * n, 2 * n + 8)
        for q in range(4):
            span = slice(q * 128, (q + 1) * 128)
            parts = []
            for c in range(KEPT):
                at = 8 * c + 2 * q
                parts.append(jnp.concatenate([arrived_ref[s, at : at + 2] for s in group], axis=0))
            for c in range(3):
                moved_ref[c, rows, span] = parts[c]
                moved_ref[4 + c, rows, span] = parts[3 + c]
            moved_ref[3, rows, span] = 1.0 - (parts[0] + parts[1] + parts[2])


def shape_of(*dims):
    return jax.ShapeDtypeStruct(dims, F32)


PARAMS = pltpu.CompilerParams(vmem_limit_bytes=32 * 1024 * 1024)


def call(body, ins, outs, scratch=(), out_specs=None):
    return pl.pallas_call(
        body,
        in_specs=list(ins),
        out_specs=out_specs or [VMEM] * len(outs),
        out_shape=list(outs),
        scratch_shapes=list(scratch),
        compiler_params=PARAMS,
        cost_estimate=pl.CostEstimate(flops=0, bytes_accessed=1000000, transcendentals=0),
    )


def shifted(value, axis, by, wrap):
    count = lax.axis_size(axis)
    pairs = [
        (source, (source + by) % count) for source in range(count) if wrap or 0 <= source + by < count
    ]
    return lax.ppermute(value, axis, pairs)


def per_device(
    phases, solutes, melt, shift_rows, flags, balance,
    stiffness, barrier, coupling, slope, diffusivity, release,
):
    slab = lax.axis_index("gz").astype(jnp.int32).reshape(1)
    small = jnp.concatenate([flags.reshape(32), shift_rows])
    plain = jnp.concatenate([melt, barrier, slope])
    table = jnp.concatenate([stiffness, coupling, diffusivity, release], axis=1)
    bulk, second, early, even, odd, strip, columns, meta = call(
        pack_z,
        [VMEM] * 2 + [SMEM] * 2,
        [
            shape_of(KEPT * ROWS + CX, 128), shape_of(KEPT * 2 * CX, 128), shape_of(STRIP + CX, 128),
            shape_of(PAIRED, 128), shape_of(PAIRED, 128), shape_of(PAIRED, 128), shape_of(ROWS, 128), shape_of(24, 128),
        ],
        [pltpu.VMEM((PAIRED, 128), F32)],
    )(phases.reshape(4, ROWS, CY), solutes.reshape(3, ROWS, CY), small, slab)
    even = lax.ppermute(even, "gz", [(0, 1), (1, 0), (2, 3), (3, 2)])
    odd = lax.ppermute(odd, "gz", [(1, 2), (2, 1)])
    above2_early, above2 = lax.cond(
        shift_rows[0] >= 7,
        lambda rows: tuple(shifted(part, "gz", -2, False) for part in rows),
        lambda rows: rows,
        (early, second),
    )
    meta, plain = lax.optimization_barrier((meta, plain))

    low, high = call(
        pack_x,
        [VMEM] * 6 + [SMEM],
        [shape_of(KEPT * X_ROWS + 4, 128)] * 2,
        [pltpu.VMEM((17 * STRIP, 128), F32)],
    )(strip, even, odd, above2_early, meta, plain.reshape(1, 11), slab)
    before = shifted(high, "gx", 1, True)
    after = shifted(low, "gx", -1, True)
    late_bulk, _ = lax.optimization_barrier((bulk, low))
    above = shifted(late_bulk, "gz", -1, False)
    turned, slots = call(
        turn_columns,
        [VMEM] * 6 + [SMEM] * 2,
        [shape_of(56, 128), jax.ShapeDtypeStruct((32,), jnp.int32)],
        [pltpu.VMEM((17 * CX, 128), F32), pltpu.VMEM((128, 128), F32), pltpu.SMEM((64,), jnp.int32)],
        out_specs=[VMEM, SMEM],
    )(columns, even, odd, above2_early, meta, plain.reshape(1, 11), slab, balance)

    face_up, face_down = call(
        pack_y, [VMEM] * 3, [shape_of(32, 128)] * 2, [pltpu.VMEM((128, 128), F32)]
    )(turned, before, after)
    left = shifted(face_up, "gy", 1, True)
    right = shifted(face_down, "gy", -1, True)

    phases_out, solutes_out, send = call(
        steps,
        [VMEM] * 11 + [SMEM] * 4,
        [shape_of(4, ROWS, CY), shape_of(3, ROWS, CY), shape_of(64, 48, 128)],
        [
            pltpu.VMEM((KEPT, 19 * CX, 128), F32),
            pltpu.VMEM((HELD, WINDOW * CX, 128), F32),
            pltpu.VMEM((128, 128), F32),
            pltpu.VMEM((128, 128), F32),
            pltpu.VMEM((HELD, 10 * CX, 128), F32),
            pltpu.VMEM((2 * HELD, 24, 128), F32),
            pltpu.VMEM((2 * HELD, 8, 128), F32),
            pltpu.VMEM((8 * ROWS, 128), F32),
        ],
    )(
        bulk, above, above2, even, odd, before, after, turned, left, right, meta, slots, slab, plain, table,
    )
    arrived = lax.all_to_all(send, ("gx", "gy"), split_axis=0, concat_axis=0, tiled=True)
    (moved,) = call(place, [VMEM], [shape_of(7, 32, 512)], [pltpu.SMEM((65,), jnp.int32)])(arrived)
    return (
        phases_out.reshape(4, CZ, CX, CY),
        solutes_out.reshape(3, CZ, CX, CY),
        jnp.transpose(moved, (1, 0, 2)),
    )


def solution(mesh):
    block = P(None, "gz", "gx", "gy")
    table = P("gz", "gx", "gy", None)
    return jax.shard_map(
        per_device,
        mesh=mesh,
        in_specs=(block, block, P(), P(), table, table, P(), P(), P(), P(), P(), P()),
        out_specs=(block, block, P(("gz", "gx", "gy"), None, None)),
        check_vma=False,
    )
```

time: 86.6 us -> 84.2 us (0.972); the launches traced: 86.3 us -> 82.8 us
  starting transfers between devices: 17.5 us -> 14.5 us
  waiting for transfers between devices: 6.86 us -> 4.81 us
  blocking collectives: 48.6 us -> 49.7 us
    ppermute x8 -> x5, starting transfers between devices: 17.5 us -> 9.66 us  [shifted(): return lax.ppermute(value, axis, pairs)]
    ppermute x8 -> x5, waiting for transfers between devices: 6.86 us -> 1.49 us  [shifted(): return lax.ppermute(value, axis, pairs)]
    ppermute x0 -> x2, starting transfers between devices: none -> 4.81 us  [the longest x1 2.57 us: per_device(): odd = lax.ppermute(odd, 'gz', [(1, 2), (2, 1)])]
    ppermute x0 -> x2, waiting for transfers between devices: none -> 3.32 us  [the longest x1 3.32 us: per_device(): odd = lax.ppermute(odd, 'gz', [(1, 2), (2, 1)])]
    concatenate x0 -> x3, other arithmetic: none -> 1.57 us  [the longest x1 0.77 us: per_device(): plain = jnp.concatenate([melt, barrier, slope])]
    all_to_all x1, blocking collectives: 48.6 us -> 49.7 us  [per_device(): lax.all_to_all(send, ('gx', 'gy'), split_axis=0, concat_axis=0, tiled=True)]
    reduce_sum x1 -> x0, other arithmetic: 0.91 us -> none  [per_device(): jnp.sum(((owner_list[:, None] == owner_list[None, :]) & (serial[None, :]...]
    unnamed x22 -> x14, local copies, waits for them, and re-layouts: 3.21 us -> 2.55 us
  transfers between devices with their start and end apart: 8 -> 7, of which waited for: 5 -> 3; matrix products, arithmetic and copies ran while one was open for 1% -> 1% of each run, Pallas kernels for 1% -> 2%
where the time goes in v3:
time: 84.2 us; the launch traced here: 82.8 us
  blocking collectives  49.7 us (59%)
  starting transfers between devices  14.5 us (17%)
  Pallas kernels  8.32 us (10%)
  waiting for transfers between devices  4.81 us (6%)
  local copies, waits for them, and re-layouts  2.55 us (3%)
  other arithmetic  1.57 us (2%)
  between operations  1.41 us (2%)
    all_to_all x1, blocking collectives, per_device(): lax.all_to_all(send, ('gx', 'gy'), split_axis=0, concat_axis=0, tiled=True)  49.7 us
    ppermute x5, starting transfers between devices, shifted(): return lax.ppermute(value, axis, pairs)  9.66 us
    pallas_call x1, Pallas kernels, per_device(): call(steps, [VMEM] * 11 + [SMEM] * 4, [shape_of(4, ROWS, CY), shape_of(3,...  4.81 us
    ppermute x1, waiting for transfers between devices, per_device(): odd = lax.ppermute(odd, 'gz', [(1, 2), (2, 1)])  3.32 us
    ppermute x1, starting transfers between devices, per_device(): odd = lax.ppermute(odd, 'gz', [(1, 2), (2, 1)])  2.57 us
    unnamed x14, local copies, waits for them, and re-layouts  2.55 us
    ppermute x1, starting transfers between devices, per_device(): even = lax.ppermute(even, 'gz', [(0, 1), (1, 0), (2, 3), (3, 2)])  2.24 us
  transfers between devices with their start and end apart: 7, of which 3 were waited for; matrix products, arithmetic and copies ran while one was open for 1% of the time, Pallas kernels for 2%

profile of v3, /device:TPU:8, one launch (start us, length us, event | category | flops | bytes accessed | tf_op | source)
XLA Modules:
  0.0 82.8 jit_solution(2455128016725087696)
XLA Ops:
  0.6 0.0 copy-start.3
  0.6 0.0 copy-start.4
  0.7 0.0 copy-start.5
  0.7 0.0 copy-start.6
  1.3 0.7 pad_add_fusion.small_ref
  2.1 0.9 %copy-done = f32[4,8,16,128]{3,2,1,0:T(8,128)S(1)} copy-done((f32[4,8,16,128]{3,2,1,0:T(8,128)S(1)}, f32[4,8,16,128]{3,2,1,0:T(8,128)}, u32[]{:S(2)}) %copy-start) | copy-done | bytes 262168
  3.0 0.9 %copy-done.1 = f32[3,8,16,128]{3,2,1,0:T(8,128)S(1)} copy-done((f32[3,8,16,128]{3,2,1,0:T(8,128)S(1)}, f32[3,8,16,128]{3,2,1,0:T(8,128)}, u32[]{:S(2)}) %copy-start.1) | copy-done | bytes 196632
  4.0 0.8 shard_map.139
  4.8 2.2 %collective-permute-start.2 = (f32[224,128]{1,0:T(8,128)S(1)}, f32[224,128]{1,0:T(8,128)S(1)}, u32[]{:S(2)}, u32[]{:S(2)}) collective-permute-start(f32[224,128]{1,0:T(8,128)S(1)} %get-tuple-element.37), channel_id=1, source_target_pairs={{0,64},{64,0},{128,192},{192,128},{1,65},{65,1},{129,193},{193,129... | collective-permute-start | bytes 344072 | tf_op jit(solution)/shard_map/ppermute | solution.py:532
  7.0 2.6 %collective-permute-start.3 = (f32[224,128]{1,0:T(8,128)S(1)}, f32[224,128]{1,0:T(8,128)S(1)}, u32[]{:S(2)}, u32[]{:S(2)}) collective-permute-start(f32[224,128]{1,0:T(8,128)S(1)} %get-tuple-element.38), channel_id=1, source_target_pairs={{64,128},{128,64},{65,129},{129,65},{66,130},{130,66},{67,131},{13... | collective-permute-start | bytes 344072 | tf_op jit(solution)/shard_map/ppermute | solution.py:533
  9.6 0.8 pad_maximum_fusion.1.plain_ref
  10.4 0.0 collective-permute-done.2.even_ref
  10.4 3.3 %collective-permute-done.3.odd_ref = f32[224,128]{1,0:T(8,128)S(1)} collective-permute-done((f32[224,128]{1,0:T(8,128)S(1)}, f32[224,128]{1,0:T(8,128)S(1)}, u32[]{:S(2)}, u32[]{:S(2)}) %collective-permute-start.3) | collective-permute-done | bytes 114720 | tf_op jit(solution)/shard_map/ppermute | solution.py:533
  13.7 0.1 shard_map.140
  13.8 1.9 %collective-permute-start.4 = (f32[784,128]{1,0:T(8,128)S(1)}, f32[784,128]{1,0:T(8,128)S(1)}, u32[]{:S(2)}, u32[]{:S(2)}) collective-permute-start(f32[784,128]{1,0:T(8,128)S(1)} %get-tuple-element.46.own_ref), channel_id=1, source_target_pairs={{64,0},{128,64},{192,128},{65,1},{129,65},{193,129},{66,2},{130,66... | collective-permute-start | bytes 1204232 | tf_op jit(solution)/shard_map/ppermute | solution.py:512
  15.8 0.7 collective-permute-start.5
  16.5 4.0 %collective-permute-start.6 = (f32[112,128]{1,0:T(8,128)S(1)}, f32[112,128]{1,0:T(8,128)S(1)}, u32[]{:S(2)}, u32[]{:S(2)}) collective-permute-start(f32[112,128]{1,0:T(8,128)S(1)} %get-tuple-element.45), channel_id=1, source_target_pairs={{0,56},{8,0},{16,8},{24,16},{32,24},{40,32},{48,40},{56,48},{1,57}... | collective-permute-start | bytes 172040 | tf_op jit(solution)/shard_map/ppermute | solution.py:512
  20.5 0.7 copy-done.2
  21.2 1.3 %shard_map.141 = (f32[56,128]{1,0:T(8,128)S(1)}, s32[32]{0:T(128)S(1)}) custom-call(f32[128,128]{1,0:T(8,128)S(1)} %get-tuple-element.49.columns_ref, f32[224,128]{1,0:T(8,128)S(1)} %collective-permute-done.2.even_ref, f32[224,128]{1,0:T(8,128)S(1)} %collective-permute-done.3.odd_ref, f32[40,128]{1,0:T(8,128)S(1)} %get-tuple-element.41.above2_ref, ...), custom_call_target="tpu_custom_call" | custom-call | bytes 1000000 | tf_op jit(solution)/shard_map/pallas_call | solution.py:552
  22.5 0.1 collective-permute-done.5.before_ref
  22.6 0.0 collective-permute-done.6.after_ref
  22.6 0.2 shard_map.142
  22.8 0.0 collective-permute-start.7
  22.8 2.9 %collective-permute-start.8 = (f32[32,128]{1,0:T(8,128)S(1)}, f32[32,128]{1,0:T(8,128)S(1)}, u32[]{:S(2)}, u32[]{:S(2)}) collective-permute-start(f32[32,128]{1,0:T(8,128)S(1)} %get-tuple-element.52), channel_id=1, source_target_pairs={{0,7},{1,0},{2,1},{3,2},{4,3},{5,4},{6,5},{7,6},{8,15},{9,8},{10,9... | collective-permute-start | bytes 49160 | tf_op jit(solution)/shard_map/ppermute | solution.py:512
  25.8 0.0 copy-done.4
  25.8 0.1 pad_maximum_fusion.table_ref
  25.8 1.3 %collective-permute-done.7.left_ref = f32[32,128]{1,0:T(8,128)S(1)} collective-permute-done((f32[32,128]{1,0:T(8,128)S(1)}, f32[32,128]{1,0:T(8,128)S(1)}, u32[]{:S(2)}, u32[]{:S(2)}) %collective-permute-start.7) | collective-permute-done | bytes 16416 | tf_op jit(solution)/shard_map/ppermute | solution.py:512
  27.2 0.0 collective-permute-done.8.right_ref
  27.2 0.0 collective-permute-done.4.above_ref
  27.2 4.8 %shard_map.143 = (f32[4,128,128]{2,1,0:T(8,128)}, f32[3,128,128]{2,1,0:T(8,128)}, f32[64,48,128]{2,1,0:T(8,128)S(1)}) custom-call(f32[784,128]{1,0:T(8,128)S(1)} %get-tuple-element.46.own_ref, f32[784,128]{1,0:T(8,128)S(1)} %collective-permute-done.4.above_ref, f32[192,128]{1,0:T(8,128)S(1)} %get-tuple-element.47.above2_ref, ...), custom_call_target="tpu_custom_call" | custom-call | bytes 1000000 | tf_op jit(solution)/shard_map/pallas_call | solution.py:566
  32.0 49.7 %all_to_all.5.arrived_ref = f32[64,48,128]{2,1,0:T(8,128)S(1)} all-to-all(f32[64,48,128]{2,1,0:T(8,128)S(1)} %get-tuple-element.56), channel_id=1, replica_groups=mesh['gz'=4,'gx'=8,'gy'=8] {'gx','gy'}, dimensions={0} | all-to-all | bytes 3145728 | tf_op jit(solution)/shard_map/all_to_all | solution.py:583
  81.7 1.1 %shard_map.144 = f32[7,32,512]{2,1,0:T(8,128)} custom-call(f32[64,48,128]{2,1,0:T(8,128)S(1)} %all_to_all.5.arrived_ref), custom_call_target="tpu_custom_call" | custom-call | bytes 1000000 | tf_op jit(solution)/shard_map/pallas_call | solution.py:584
  (7 shorter events, 0.0 us)
Async XLA Ops:
  0.6 25.1 %copy-start.3 = (f32[4,3]{1,0:T(4,128)S(1)}, f32[4,3]{1,0:T(4,128)}, u32[]{:S(2)}) copy-start(f32[4,3]{1,0:T(4,128)} %param.25) | copy-start | bytes 148
  0.6 25.1 %copy-start.4 = (f32[4,3]{1,0:T(4,128)S(1)}, f32[4,3]{1,0:T(4,128)}, u32[]{:S(2)}) copy-start(f32[4,3]{1,0:T(4,128)} %param.24) | copy-start | bytes 148
  0.7 25.1 %copy-start.5 = (f32[4,3]{1,0:T(4,128)S(1)}, f32[4,3]{1,0:T(4,128)}, u32[]{:S(2)}) copy-start(f32[4,3]{1,0:T(4,128)} %param.22) | copy-start | bytes 148
  0.7 25.1 %copy-start.6 = (f32[4,3]{1,0:T(4,128)S(1)}, f32[4,3]{1,0:T(4,128)}, u32[]{:S(2)}) copy-start(f32[4,3]{1,0:T(4,128)} %param.20) | copy-start | bytes 148
  2.1 0.9 %copy-start = (f32[4,8,16,128]{3,2,1,0:T(8,128)S(1)}, f32[4,8,16,128]{3,2,1,0:T(8,128)}, u32[]{:S(2)}) copy-start(f32[4,8,16,128]{3,2,1,0:T(8,128)} %param.14) | copy-start | bytes 786436
  3.0 0.9 %copy-start.1 = (f32[3,8,16,128]{3,2,1,0:T(8,128)S(1)}, f32[3,8,16,128]{3,2,1,0:T(8,128)}, u32[]{:S(2)}) copy-start(f32[3,8,16,128]{3,2,1,0:T(8,128)} %param.15) | copy-start | bytes 589828
  4.8 5.6 %collective-permute-start.2 = (f32[224,128]{1,0:T(8,128)S(1)}, f32[224,128]{1,0:T(8,128)S(1)}, u32[]{:S(2)}, u32[]{:S(2)}) collective-permute-start(f32[224,128]{1,0:T(8,128)S(1)} %get-tuple-element.37), channel_id=1, source_target_pairs={{0,64},{64,0},{128,192},{192,128},{1,65},{65,1},{129,193},{193,129... | collective-permute-start | bytes 344072 | tf_op jit(solution)/shard_map/ppermute | solution.py:532
  7.0 6.7 %collective-permute-start.3 = (f32[224,128]{1,0:T(8,128)S(1)}, f32[224,128]{1,0:T(8,128)S(1)}, u32[]{:S(2)}, u32[]{:S(2)}) collective-permute-start(f32[224,128]{1,0:T(8,128)S(1)} %get-tuple-element.38), channel_id=1, source_target_pairs={{64,128},{128,64},{65,129},{129,65},{66,130},{130,66},{67,131},{13... | collective-permute-start | bytes 344072 | tf_op jit(solution)/shard_map/ppermute | solution.py:533
  13.8 13.4 %collective-permute-start.4 = (f32[784,128]{1,0:T(8,128)S(1)}, f32[784,128]{1,0:T(8,128)S(1)}, u32[]{:S(2)}, u32[]{:S(2)}) collective-permute-start(f32[784,128]{1,0:T(8,128)S(1)} %get-tuple-element.46.own_ref), channel_id=1, source_target_pairs={{64,0},{128,64},{192,128},{65,1},{129,65},{193,129},{66,2},{130,66... | collective-permute-start | bytes 1204232 | tf_op jit(solution)/shard_map/ppermute | solution.py:512
  15.8 6.8 %collective-permute-start.5 = (f32[112,128]{1,0:T(8,128)S(1)}, f32[112,128]{1,0:T(8,128)S(1)}, u32[]{:S(2)}, u32[]{:S(2)}) collective-permute-start(f32[112,128]{1,0:T(8,128)S(1)} %get-tuple-element.48), channel_id=1, source_target_pairs={{0,8},{8,16},{16,24},{24,32},{32,40},{40,48},{48,56},{56,0},{1,9},... | collective-permute-start | bytes 172040 | tf_op jit(solution)/shard_map/ppermute | solution.py:512
  16.5 6.1 %collective-permute-start.6 = (f32[112,128]{1,0:T(8,128)S(1)}, f32[112,128]{1,0:T(8,128)S(1)}, u32[]{:S(2)}, u32[]{:S(2)}) collective-permute-start(f32[112,128]{1,0:T(8,128)S(1)} %get-tuple-element.45), channel_id=1, source_target_pairs={{0,56},{8,0},{16,8},{24,16},{32,24},{40,32},{48,40},{56,48},{1,57}... | collective-permute-start | bytes 172040 | tf_op jit(solution)/shard_map/ppermute | solution.py:512
  20.5 0.7 copy-start.2
  22.8 4.4 %collective-permute-start.7 = (f32[32,128]{1,0:T(8,128)S(1)}, f32[32,128]{1,0:T(8,128)S(1)}, u32[]{:S(2)}, u32[]{:S(2)}) collective-permute-start(f32[32,128]{1,0:T(8,128)S(1)} %get-tuple-element.51), channel_id=1, source_target_pairs={{0,1},{1,2},{2,3},{3,4},{4,5},{5,6},{6,7},{7,0},{8,9},{9,10},{10,1... | collective-permute-start | bytes 49160 | tf_op jit(solution)/shard_map/ppermute | solution.py:512
  22.8 4.4 %collective-permute-start.8 = (f32[32,128]{1,0:T(8,128)S(1)}, f32[32,128]{1,0:T(8,128)S(1)}, u32[]{:S(2)}, u32[]{:S(2)}) collective-permute-start(f32[32,128]{1,0:T(8,128)S(1)} %get-tuple-element.52), channel_id=1, source_target_pairs={{0,7},{1,0},{2,1},{3,2},{4,3},{5,4},{6,5},{7,6},{8,15},{9,8},{10,9... | collective-permute-start | bytes 49160 | tf_op jit(solution)/shard_map/ppermute | solution.py:512

commit v4 on v3

--- a/solution.py
+++ b/solution.py
@@ -51,7 +51,7 @@
 
 def pack_z(
     phases_ref, solutes_ref, small_ref, slab_ref,
-    bulk_ref, second_ref, early_ref, even_ref, odd_ref, strip_ref, columns_ref, meta_ref,
+    bulk_ref, second_ref, even_ref, odd_ref, strip_ref, columns_ref, meta_ref,
     last_ref,
 ):
     flags = jnp.concatenate([flag_row(small_ref, b) for b in range(2)], axis=0)
@@ -66,13 +66,11 @@
         last_ref[c * CX : (c + 1) * CX] = bulk_ref[c * ROWS + 7 * CX : (c + 1) * ROWS]
         for n, x in enumerate(LAYERS):
             strip_ref[pl.ds(n * KEPT + c, 8, stride=STRIP)] = bulk_ref[pl.ds(c * ROWS + x, 8, stride=CX)]
-            early_ref[n * KEPT + c : n * KEPT + c + 1] = bulk_ref[c * ROWS + x : c * ROWS + x + 1]
     flags = pltpu.roll(flags, 25, 1)
     flag_lane = (lanes_of(CX) == 24) | (lanes_of(CX) == 25)
     for z in range(CZ):
         packed = gather(CX, lambda c: bulk_ref[c * ROWS + z * CX : c * ROWS + (z + 1) * CX])
         columns_ref[z * CX : (z + 1) * CX] = jnp.where(flag_lane, flags, packed)
-    early_ref[STRIP : STRIP + CX] = columns_ref[0:CX]
     strip_ref[8 * STRIP : PAIRED] = columns_ref[...].T[0:32]
     is_even = (slab_ref[0] & 1) == 0
     last_ref[(KEPT + 1) * CX : PAIRED] = jnp.zeros((PAIRED - (KEPT + 1) * CX, 128), F32)
@@ -104,7 +102,8 @@
         rows = slice(z * STRIP, (z + 1) * STRIP)
         here = jnp.where((slab & 1) == 0, even_ref[rows], odd_ref[rows])
         raw_ref[(8 + z) * STRIP : (9 + z) * STRIP] = jnp.where(slab == 3, fresh, here)
-    raw_ref[16 * STRIP : 17 * STRIP] = above2_ref[0:STRIP]
+    for n, x in enumerate(LAYERS):
+        raw_ref[16 * STRIP + n * KEPT : 16 * STRIP + (n + 1) * KEPT] = above2_ref[pl.ds(x, KEPT, stride=2 * CX)]
 
     @pl.when(slab >= 2)
     def _():
@@ -150,7 +149,9 @@
         for z in range(CZ):
             raw_ref[ROWS + z * CX : ROWS + (z + 1) * CX] = fresh
 
-    raw_ref[2 * ROWS : 2 * ROWS + CX] = jnp.where(slab >= 2, fresh, above2_ref[STRIP : STRIP + CX])
+    raw_ref[2 * ROWS : 2 * ROWS + CX] = jnp.where(
+        slab >= 2, fresh, gather(CX, lambda c: above2_ref[2 * c * CX : (2 * c + 1) * CX])
+    )
 
     def rows_at(row):
         return raw_ref[pl.ds(pl.multiple_of(row * CX, CX), CX)]
@@ -520,22 +521,19 @@
     small = jnp.concatenate([flags.reshape(32), shift_rows])
     plain = jnp.concatenate([melt, barrier, slope])
     table = jnp.concatenate([stiffness, coupling, diffusivity, release], axis=1)
-    bulk, second, early, even, odd, strip, columns, meta = call(
+    bulk, second, even, odd, strip, columns, meta = call(
         pack_z,
         [VMEM] * 2 + [SMEM] * 2,
         [
-            shape_of(KEPT * ROWS + CX, 128), shape_of(KEPT * 2 * CX, 128), shape_of(STRIP + CX, 128),
+            shape_of(KEPT * ROWS + CX, 128), shape_of(KEPT * 2 * CX, 128),
             shape_of(PAIRED, 128), shape_of(PAIRED, 128), shape_of(PAIRED, 128), shape_of(ROWS, 128), shape_of(24, 128),
         ],
         [pltpu.VMEM((PAIRED, 128), F32)],
     )(phases.reshape(4, ROWS, CY), solutes.reshape(3, ROWS, CY), small, slab)
     even = lax.ppermute(even, "gz", [(0, 1), (1, 0), (2, 3), (3, 2)])
     odd = lax.ppermute(odd, "gz", [(1, 2), (2, 1)])
-    above2_early, above2 = lax.cond(
-        shift_rows[0] >= 7,
-        lambda rows: tuple(shifted(part, "gz", -2, False) for part in rows),
-        lambda rows: rows,
-        (early, second),
+    above2 = lax.cond(
+        shift_rows[0] >= 7, lambda rows: shifted(rows, "gz", -2, False), lambda rows: rows, second
     )
     meta, plain = lax.optimization_barrier((meta, plain))
 
@@ -544,7 +542,7 @@
         [VMEM] * 6 + [SMEM],
         [shape_of(KEPT * X_ROWS + 4, 128)] * 2,
         [pltpu.VMEM((17 * STRIP, 128), F32)],
-    )(strip, even, odd, above2_early, meta, plain.reshape(1, 11), slab)
+    )(strip, even, odd, above2, meta, plain.reshape(1, 11), slab)
     before = shifted(high, "gx", 1, True)
     after = shifted(low, "gx", -1, True)
     late_bulk, _ = lax.optimization_barrier((bulk, low))
@@ -555,7 +553,7 @@
         [shape_of(56, 128), jax.ShapeDtypeStruct((32,), jnp.int32)],
         [pltpu.VMEM((17 * CX, 128), F32), pltpu.VMEM((128, 128), F32), pltpu.SMEM((64,), jnp.int32)],
         out_specs=[VMEM, SMEM],
-    )(columns, even, odd, above2_early, meta, plain.reshape(1, 11), slab, balance)
+    )(columns, even, odd, above2, meta, plain.reshape(1, 11), slab, balance)
 
     face_up, face_down = call(
         pack_y, [VMEM] * 3, [shape_of(32, 128)] * 2, [pltpu.VMEM((128, 128), F32)]

time: 84.2 us -> 84.2 us (level)
  no operation moved by 1% of the time
where the time goes in v4:
time: 84.2 us; the launch traced here: 82.8 us
  blocking collectives  49.7 us (59%)
  starting transfers between devices  14.5 us (17%)
  Pallas kernels  8.31 us (10%)
  waiting for transfers between devices  4.81 us (6%)
  local copies, waits for them, and re-layouts  2.55 us (3%)
  other arithmetic  1.57 us (2%)
  between operations  1.41 us (2%)
    all_to_all x1, blocking collectives, per_device(): lax.all_to_all(send, ('gx', 'gy'), split_axis=0, concat_axis=0, tiled=True)  49.7 us
    ppermute x5, starting transfers between devices, shifted(): return lax.ppermute(value, axis, pairs)  9.66 us
    pallas_call x1, Pallas kernels, per_device(): call(steps, [VMEM] * 11 + [SMEM] * 4, [shape_of(4, ROWS, CY), shape_of(3,...  4.81 us
    ppermute x1, waiting for transfers between devices, per_device(): odd = lax.ppermute(odd, 'gz', [(1, 2), (2, 1)])  3.32 us
    ppermute x1, starting transfers between devices, per_device(): odd = lax.ppermute(odd, 'gz', [(1, 2), (2, 1)])  2.57 us
    unnamed x14, local copies, waits for them, and re-layouts  2.55 us
    ppermute x1, starting transfers between devices, per_device(): even = lax.ppermute(even, 'gz', [(0, 1), (1, 0), (2, 3), (3, 2)])  2.24 us
  transfers between devices with their start and end apart: 7, of which 3 were waited for; matrix products, arithmetic and copies ran while one was open for 1% of the time, Pallas kernels for 2%

profile of v4, /device:TPU:8, one launch (start us, length us, event | category | flops | bytes accessed | tf_op | source)
XLA Modules:
  0.0 82.8 jit_solution(1801885393806465608)
XLA Ops:
  0.6 0.0 copy-start.3
  0.6 0.0 copy-start.4
  0.7 0.0 copy-start.5
  0.7 0.0 copy-start.6
  1.3 0.7 pad_add_fusion.small_ref
  2.1 0.9 %copy-done = f32[4,8,16,128]{3,2,1,0:T(8,128)S(1)} copy-done((f32[4,8,16,128]{3,2,1,0:T(8,128)S(1)}, f32[4,8,16,128]{3,2,1,0:T(8,128)}, u32[]{:S(2)}) %copy-start) | copy-done | bytes 262168
  3.0 0.9 %copy-done.1 = f32[3,8,16,128]{3,2,1,0:T(8,128)S(1)} copy-done((f32[3,8,16,128]{3,2,1,0:T(8,128)S(1)}, f32[3,8,16,128]{3,2,1,0:T(8,128)}, u32[]{:S(2)}) %copy-start.1) | copy-done | bytes 196632
  4.0 0.8 shard_map.139
  4.8 2.2 %collective-permute-start.1 = (f32[224,128]{1,0:T(8,128)S(1)}, f32[224,128]{1,0:T(8,128)S(1)}, u32[]{:S(2)}, u32[]{:S(2)}) collective-permute-start(f32[224,128]{1,0:T(8,128)S(1)} %get-tuple-element.29), channel_id=1, source_target_pairs={{0,64},{64,0},{128,192},{192,128},{1,65},{65,1},{129,193},{193,129... | collective-permute-start | bytes 344072 | tf_op jit(solution)/shard_map/ppermute | solution.py:533
  7.0 2.6 %collective-permute-start.2 = (f32[224,128]{1,0:T(8,128)S(1)}, f32[224,128]{1,0:T(8,128)S(1)}, u32[]{:S(2)}, u32[]{:S(2)}) collective-permute-start(f32[224,128]{1,0:T(8,128)S(1)} %get-tuple-element.30), channel_id=1, source_target_pairs={{64,128},{128,64},{65,129},{129,65},{66,130},{130,66},{67,131},{13... | collective-permute-start | bytes 344072 | tf_op jit(solution)/shard_map/ppermute | solution.py:534
  9.6 0.8 pad_maximum_fusion.1.plain_ref
  10.3 0.0 collective-permute-done.1.even_ref
  10.4 3.3 %collective-permute-done.2.odd_ref = f32[224,128]{1,0:T(8,128)S(1)} collective-permute-done((f32[224,128]{1,0:T(8,128)S(1)}, f32[224,128]{1,0:T(8,128)S(1)}, u32[]{:S(2)}, u32[]{:S(2)}) %collective-permute-start.2) | collective-permute-done | bytes 114720 | tf_op jit(solution)/shard_map/ppermute | solution.py:534
  13.7 0.1 shard_map.140
  13.8 1.9 %collective-permute-start.3 = (f32[784,128]{1,0:T(8,128)S(1)}, f32[784,128]{1,0:T(8,128)S(1)}, u32[]{:S(2)}, u32[]{:S(2)}) collective-permute-start(f32[784,128]{1,0:T(8,128)S(1)} %get-tuple-element.36.own_ref), channel_id=1, source_target_pairs={{64,0},{128,64},{192,128},{65,1},{129,65},{193,129},{66,2},{130,66... | collective-permute-start | bytes 1204232 | tf_op jit(solution)/shard_map/ppermute | solution.py:513
  15.7 0.7 collective-permute-start.4
  16.5 4.0 %collective-permute-start.5 = (f32[112,128]{1,0:T(8,128)S(1)}, f32[112,128]{1,0:T(8,128)S(1)}, u32[]{:S(2)}, u32[]{:S(2)}) collective-permute-start(f32[112,128]{1,0:T(8,128)S(1)} %get-tuple-element.35), channel_id=1, source_target_pairs={{0,56},{8,0},{16,8},{24,16},{32,24},{40,32},{48,40},{56,48},{1,57}... | collective-permute-start | bytes 172040 | tf_op jit(solution)/shard_map/ppermute | solution.py:513
  20.5 0.7 copy-done.2
  21.2 1.3 %shard_map.141 = (f32[56,128]{1,0:T(8,128)S(1)}, s32[32]{0:T(128)S(1)}) custom-call(f32[128,128]{1,0:T(8,128)S(1)} %get-tuple-element.38.columns_ref, f32[224,128]{1,0:T(8,128)S(1)} %collective-permute-done.1.even_ref, f32[224,128]{1,0:T(8,128)S(1)} %collective-permute-done.2.odd_ref, f32[192,128]{1,0:T(8,128)S(1)} %get-tuple-element.46.above2_ref, ...), custom_call_target="tpu_custom_call" | custom-call | bytes 1000000 | tf_op jit(solution)/shard_map/pallas_call | solution.py:550
  22.5 0.1 collective-permute-done.4.before_ref
  22.6 0.0 collective-permute-done.5.after_ref
  22.6 0.2 shard_map.142
  22.8 0.0 collective-permute-start.6
  22.8 2.9 %collective-permute-start.7 = (f32[32,128]{1,0:T(8,128)S(1)}, f32[32,128]{1,0:T(8,128)S(1)}, u32[]{:S(2)}, u32[]{:S(2)}) collective-permute-start(f32[32,128]{1,0:T(8,128)S(1)} %get-tuple-element.41), channel_id=1, source_target_pairs={{0,7},{1,0},{2,1},{3,2},{4,3},{5,4},{6,5},{7,6},{8,15},{9,8},{10,9... | collective-permute-start | bytes 49160 | tf_op jit(solution)/shard_map/ppermute | solution.py:513
  25.7 0.0 copy-done.3
  25.8 0.1 pad_maximum_fusion.table_ref
  25.8 1.3 %collective-permute-done.6.left_ref = f32[32,128]{1,0:T(8,128)S(1)} collective-permute-done((f32[32,128]{1,0:T(8,128)S(1)}, f32[32,128]{1,0:T(8,128)S(1)}, u32[]{:S(2)}, u32[]{:S(2)}) %collective-permute-start.6) | collective-permute-done | bytes 16416 | tf_op jit(solution)/shard_map/ppermute | solution.py:513
  27.2 0.0 collective-permute-done.7.right_ref
  27.2 0.0 collective-permute-done.3.above_ref
  27.2 4.8 %shard_map.143 = (f32[4,128,128]{2,1,0:T(8,128)}, f32[3,128,128]{2,1,0:T(8,128)}, f32[64,48,128]{2,1,0:T(8,128)S(1)}) custom-call(f32[784,128]{1,0:T(8,128)S(1)} %get-tuple-element.36.own_ref, f32[784,128]{1,0:T(8,128)S(1)} %collective-permute-done.3.above_ref, f32[192,128]{1,0:T(8,128)S(1)} %get-tuple-element.46.above2_ref, ...), custom_call_target="tpu_custom_call" | custom-call | bytes 1000000 | tf_op jit(solution)/shard_map/pallas_call | solution.py:564
  32.0 49.7 %all_to_all.5.arrived_ref = f32[64,48,128]{2,1,0:T(8,128)S(1)} all-to-all(f32[64,48,128]{2,1,0:T(8,128)S(1)} %get-tuple-element.45), channel_id=1, replica_groups=mesh['gz'=4,'gx'=8,'gy'=8] {'gx','gy'}, dimensions={0} | all-to-all | bytes 3145728 | tf_op jit(solution)/shard_map/all_to_all | solution.py:581
  81.7 1.1 %shard_map.144 = f32[7,32,512]{2,1,0:T(8,128)} custom-call(f32[64,48,128]{2,1,0:T(8,128)S(1)} %all_to_all.5.arrived_ref), custom_call_target="tpu_custom_call" | custom-call | bytes 1000000 | tf_op jit(solution)/shard_map/pallas_call | solution.py:582
  (7 shorter events, 0.0 us)
Async XLA Ops:
  0.6 25.1 %copy-start.3 = (f32[4,3]{1,0:T(4,128)S(1)}, f32[4,3]{1,0:T(4,128)}, u32[]{:S(2)}) copy-start(f32[4,3]{1,0:T(4,128)} %param.25) | copy-start | bytes 148
  0.6 25.1 %copy-start.4 = (f32[4,3]{1,0:T(4,128)S(1)}, f32[4,3]{1,0:T(4,128)}, u32[]{:S(2)}) copy-start(f32[4,3]{1,0:T(4,128)} %param.24) | copy-start | bytes 148
  0.7 25.1 %copy-start.5 = (f32[4,3]{1,0:T(4,128)S(1)}, f32[4,3]{1,0:T(4,128)}, u32[]{:S(2)}) copy-start(f32[4,3]{1,0:T(4,128)} %param.22) | copy-start | bytes 148
  0.7 25.1 %copy-start.6 = (f32[4,3]{1,0:T(4,128)S(1)}, f32[4,3]{1,0:T(4,128)}, u32[]{:S(2)}) copy-start(f32[4,3]{1,0:T(4,128)} %param.20) | copy-start | bytes 148
  2.1 0.9 %copy-start = (f32[4,8,16,128]{3,2,1,0:T(8,128)S(1)}, f32[4,8,16,128]{3,2,1,0:T(8,128)}, u32[]{:S(2)}) copy-start(f32[4,8,16,128]{3,2,1,0:T(8,128)} %param.14) | copy-start | bytes 786436
  3.0 0.9 %copy-start.1 = (f32[3,8,16,128]{3,2,1,0:T(8,128)S(1)}, f32[3,8,16,128]{3,2,1,0:T(8,128)}, u32[]{:S(2)}) copy-start(f32[3,8,16,128]{3,2,1,0:T(8,128)} %param.15) | copy-start | bytes 589828
  4.8 5.6 %collective-permute-start.1 = (f32[224,128]{1,0:T(8,128)S(1)}, f32[224,128]{1,0:T(8,128)S(1)}, u32[]{:S(2)}, u32[]{:S(2)}) collective-permute-start(f32[224,128]{1,0:T(8,128)S(1)} %get-tuple-element.29), channel_id=1, source_target_pairs={{0,64},{64,0},{128,192},{192,128},{1,65},{65,1},{129,193},{193,129... | collective-permute-start | bytes 344072 | tf_op jit(solution)/shard_map/ppermute | solution.py:533
  7.0 6.7 %collective-permute-start.2 = (f32[224,128]{1,0:T(8,128)S(1)}, f32[224,128]{1,0:T(8,128)S(1)}, u32[]{:S(2)}, u32[]{:S(2)}) collective-permute-start(f32[224,128]{1,0:T(8,128)S(1)} %get-tuple-element.30), channel_id=1, source_target_pairs={{64,128},{128,64},{65,129},{129,65},{66,130},{130,66},{67,131},{13... | collective-permute-start | bytes 344072 | tf_op jit(solution)/shard_map/ppermute | solution.py:534
  13.8 13.4 %collective-permute-start.3 = (f32[784,128]{1,0:T(8,128)S(1)}, f32[784,128]{1,0:T(8,128)S(1)}, u32[]{:S(2)}, u32[]{:S(2)}) collective-permute-start(f32[784,128]{1,0:T(8,128)S(1)} %get-tuple-element.36.own_ref), channel_id=1, source_target_pairs={{64,0},{128,64},{192,128},{65,1},{129,65},{193,129},{66,2},{130,66... | collective-permute-start | bytes 1204232 | tf_op jit(solution)/shard_map/ppermute | solution.py:513
  15.7 6.8 %collective-permute-start.4 = (f32[112,128]{1,0:T(8,128)S(1)}, f32[112,128]{1,0:T(8,128)S(1)}, u32[]{:S(2)}, u32[]{:S(2)}) collective-permute-start(f32[112,128]{1,0:T(8,128)S(1)} %get-tuple-element.37), channel_id=1, source_target_pairs={{0,8},{8,16},{16,24},{24,32},{32,40},{40,48},{48,56},{56,0},{1,9},... | collective-permute-start | bytes 172040 | tf_op jit(solution)/shard_map/ppermute | solution.py:513
  16.5 6.1 %collective-permute-start.5 = (f32[112,128]{1,0:T(8,128)S(1)}, f32[112,128]{1,0:T(8,128)S(1)}, u32[]{:S(2)}, u32[]{:S(2)}) collective-permute-start(f32[112,128]{1,0:T(8,128)S(1)} %get-tuple-element.35), channel_id=1, source_target_pairs={{0,56},{8,0},{16,8},{24,16},{32,24},{40,32},{48,40},{56,48},{1,57}... | collective-permute-start | bytes 172040 | tf_op jit(solution)/shard_map/ppermute | solution.py:513
  20.5 0.7 copy-start.2
  22.8 4.4 %collective-permute-start.6 = (f32[32,128]{1,0:T(8,128)S(1)}, f32[32,128]{1,0:T(8,128)S(1)}, u32[]{:S(2)}, u32[]{:S(2)}) collective-permute-start(f32[32,128]{1,0:T(8,128)S(1)} %get-tuple-element.40), channel_id=1, source_target_pairs={{0,1},{1,2},{2,3},{3,4},{4,5},{5,6},{6,7},{7,0},{8,9},{9,10},{10,1... | collective-permute-start | bytes 49160 | tf_op jit(solution)/shard_map/ppermute | solution.py:513
  22.8 4.4 %collective-permute-start.7 = (f32[32,128]{1,0:T(8,128)S(1)}, f32[32,128]{1,0:T(8,128)S(1)}, u32[]{:S(2)}, u32[]{:S(2)}) collective-permute-start(f32[32,128]{1,0:T(8,128)S(1)} %get-tuple-element.41), channel_id=1, source_target_pairs={{0,7},{1,0},{2,1},{3,2},{4,3},{5,4},{6,5},{7,6},{8,15},{9,8},{10,9... | collective-permute-start | bytes 49160 | tf_op jit(solution)/shard_map/ppermute | solution.py:513
